TPU v7x, 256 devices: a whole 4x4x8 slice. The times are simulated.
256 devices in a mesh: seq: 64 (over x, z_hi, y, core), chan: 4 (over z_lo).
Axes of the slice: x: 4, y: 4, z: 8 (z_hi: 2, z_lo: 4; z = z_hi * 4 + z_lo), core: 2. Of those that a mesh axis runs over, the one named last changes fastest.
Arguments:
- values: bfloat16 [8192, 4096], P('seq', 'chan'), may hold values from -6 to 6
- gates: bfloat16 [8192, 4096], P('seq', 'chan'), may hold values from -6 to 6
- grad_out: float32 [8192, 4096], P('seq', 'chan'), may hold values from -6 to 6
- filter_raw: bfloat16 [8192, 1024], P('seq'), may hold values from -6 to 6
- skip_gain: float32 [4096], P('chan'), may hold values from 0.5 to 1.5
Outputs:
- value_grad: bfloat16 [8192, 4096], P('seq', 'chan')
- gate_grad: bfloat16 [8192, 4096], P('seq', 'chan')
- filter_grad: float32 [8192, 1024], P('seq', 'chan')
All inputs are finite; a program needn't handle non-finite values.
Results may differ from a plain program's by a relative error of at most 0.01.
Values may be sent and summed in bfloat16 or wider, within the bound.
No kernel may reach another device: no remote copies, remote signals or barrier semaphores. Data moves between devices by JAX's collectives and lax.ppermute only.
A program may use at most 64 MiB of HBM per device.

v0:
```python
import math

import jax
import jax.numpy as jnp
from jax import lax
from jax.sharding import PartitionSpec as P

EXACT = lax.Precision.HIGHEST


def phase_pair(count_rows, count_cols, period, col_start):
    left = lax.iota(jnp.int32, count_rows)[:, None]
    right = (lax.iota(jnp.int32, count_cols) + col_start)[None, :]
    turned = (left * right % period).astype(jnp.float32) * (2.0 * math.pi / period)
    return (jnp.cos(turned), jnp.sin(turned))


def forward_spectrum(signal, phases):
    block_cos, block_sin, twist_cos, twist_sin, row_cos, row_sin = phases
    tok_rows, width = signal.shape
    outgoing = signal.reshape(1, tok_rows, width)
    columns = lax.all_to_all(outgoing, "seq", split_axis=1, concat_axis=0, tiled=True).astype(
        jnp.float32
    )
    real_part = jnp.einsum("ka,ajc->kjc", block_cos, columns, precision=EXACT)
    imag_part = -jnp.einsum("ka,ajc->kjc", block_sin, columns, precision=EXACT)
    twist_c = twist_cos[:, :, None]
    twist_s = twist_sin[:, :, None]
    stacked = jnp.stack(
        [real_part * twist_c + imag_part * twist_s, imag_part * twist_c - real_part * twist_s]
    )
    received = lax.all_to_all(stacked, "seq", split_axis=1, concat_axis=2, tiled=True)
    real_in = received[0]
    imag_in = received[1]
    real_out = jnp.einsum("kj,bjc->bkc", row_cos, real_in, precision=EXACT) + jnp.einsum(
        "kj,bjc->bkc", row_sin, imag_in, precision=EXACT
    )
    imag_out = jnp.einsum("kj,bjc->bkc", row_cos, imag_in, precision=EXACT) - jnp.einsum(
        "kj,bjc->bkc", row_sin, real_in, precision=EXACT
    )
    return jnp.stack([real_out, imag_out])


def inverse_signal(spectrum, phases, period_len):
    block_cos, block_sin, twist_cos, twist_sin, row_cos, row_sin = phases
    real_in = spectrum[0]
    imag_in = spectrum[1]
    real_rows = jnp.einsum("kj,bkc->bjc", row_cos, real_in, precision=EXACT) - jnp.einsum(
        "kj,bkc->bjc", row_sin, imag_in, precision=EXACT
    )
    imag_rows = jnp.einsum("kj,bkc->bjc", row_cos, imag_in, precision=EXACT) + jnp.einsum(
        "kj,bkc->bjc", row_sin, real_in, precision=EXACT
    )
    stacked = jnp.stack([real_rows, imag_rows])
    twist_c = twist_cos[:, :, None]
    twist_s = twist_sin[:, :, None]
    received = lax.all_to_all(stacked, "seq", split_axis=2, concat_axis=1, tiled=True)
    real_part = received[0] * twist_c - received[1] * twist_s
    imag_part = received[1] * twist_c + received[0] * twist_s
    summed = jnp.einsum("ka,kjc->ajc", block_cos, real_part, precision=EXACT) - jnp.einsum(
        "ka,kjc->ajc", block_sin, imag_part, precision=EXACT
    )
    blocks = summed * (1.0 / period_len)
    returned = lax.all_to_all(blocks, "seq", split_axis=0, concat_axis=1, tiled=True)
    return returned.reshape(returned.shape[1], returned.shape[2])


def complex_product(left, right):
    return jnp.stack(
        [left[0] * right[0] - left[1] * right[1], left[0] * right[1] + left[1] * right[0]]
    )


def conj_product(left, right):
    return jnp.stack(
        [left[0] * right[0] + left[1] * right[1], left[0] * right[1] - left[1] * right[0]]
    )


def local(values, gates, grad_out, filter_raw, skip_gain):
    tok_rows, width = values.shape
    seq_count = lax.axis_size("seq")
    col_rows = tok_rows // seq_count
    period_len = 2 * seq_count * tok_rows
    rank_seq = lax.axis_index("seq")
    block_cos, block_sin = phase_pair(2 * seq_count, seq_count, 2 * seq_count, 0)
    twist_cos, twist_sin = phase_pair(2 * seq_count, col_rows, period_len, rank_seq * col_rows)
    row_cos, row_sin = phase_pair(tok_rows, tok_rows, tok_rows, 0)
    phases = (block_cos, block_sin, twist_cos, twist_sin, row_cos, row_sin)
    scale = 1.0 / math.sqrt(seq_count * tok_rows)
    gate_term = (grad_out * gates.astype(jnp.float32)).astype(jnp.bfloat16)
    spec_values = forward_spectrum(values, phases)
    spec_gate = forward_spectrum(gate_term, phases)
    spec_filter = forward_spectrum(filter_raw, phases)
    conv_spec = complex_product(spec_filter, spec_values)
    value_spec = conj_product(spec_filter, spec_gate)
    filter_spec = conj_product(spec_values, spec_gate)
    conv = inverse_signal(conv_spec, phases, period_len) * scale
    back_v = inverse_signal(value_spec, phases, period_len) * scale
    terms = inverse_signal(filter_spec, phases, period_len)
    filter_grad = lax.psum_scatter(terms, "chan", scatter_dimension=1, tiled=True) * scale
    mixed = conv + skip_gain[None, :] * values.astype(jnp.float32)
    gate_grad = (grad_out * mixed).astype(jnp.bfloat16)
    value_grad = (back_v + skip_gain[None, :] * gate_term.astype(jnp.float32)).astype(jnp.bfloat16)
    return (value_grad, gate_grad, filter_grad)


def solution(mesh):
    in_specs = (P("seq", "chan"), P("seq", "chan"), P("seq", "chan"), P("seq", None), P("chan"))
    out_specs = (P("seq", "chan"), P("seq", "chan"), P("seq", "chan"))
    return jax.shard_map(local, mesh=mesh, in_specs=in_specs, out_specs=out_specs, check_vma=False)
```

profile of v0, /device:TPU:1, one launch (start us, length us, event | category | flops | bytes accessed | tf_op | source)
XLA Modules:
  0.0 554.9 jit_solution(3710048186346343736)
XLA Ops:
  12.1 15.6 %all-to-all-start.6 = ((bf16[64,2,1024]{2,1,0:T(2,128)(2,1)}), bf16[64,2,1024]{2,1,0:T(2,128)(2,1)S(1)}, u32[]{:S(2)}, u32[]{:S(2)}) async-start(bf16[64,2,1024]{2,1,0:T(2,128)(2,1)} %reshape.140), calls=%async_computation.6 | async-start | bytes 524288 | tf_op jit(solution)/shard_map/all_to_all | solution.py:22
  28.2 2.2 reduce.7
  31.6 2.2 reduce.8
  34.7 6.8 %all-to-all-done.6 = bf16[64,2,1024]{2,1,0:T(2,128)(2,1)S(1)} async-done(((bf16[64,2,1024]{2,1,0:T(2,128)(2,1)}), bf16[64,2,1024]{2,1,0:T(2,128)(2,1)S(1)}, u32[]{:S(2)}, u32[]{:S(2)}) %all-to-all-start.6) | async-done | bytes 262176 | tf_op jit(solution)/shard_map/all_to_all | solution.py:22
  41.5 6.0 %all-to-all-start.2 = ((bf16[64,2,1024]{2,1,0:T(2,128)(2,1)}), bf16[64,2,1024]{2,1,0:T(2,128)(2,1)S(1)}, u32[]{:S(2)}, u32[]{:S(2)}) async-start(bf16[64,2,1024]{2,1,0:T(2,128)(2,1)} %reshape.138), calls=%async_computation.2 | async-start | bytes 524288 | tf_op jit(solution)/shard_map/all_to_all | solution.py:22
  50.8 10.5 %all-to-all-done.2 = bf16[64,2,1024]{2,1,0:T(2,128)(2,1)S(1)} async-done(((bf16[64,2,1024]{2,1,0:T(2,128)(2,1)}), bf16[64,2,1024]{2,1,0:T(2,128)(2,1)S(1)}, u32[]{:S(2)}, u32[]{:S(2)}) %all-to-all-start.2) | async-done | bytes 262176 | tf_op jit(solution)/shard_map/all_to_all | solution.py:22
  61.3 5.9 %all-to-all-start = ((bf16[64,2,1024]{2,1,0:T(2,128)(2,1)}), bf16[64,2,1024]{2,1,0:T(2,128)(2,1)}, u32[]{:S(2)}, u32[]{:S(2)}) async-start(bf16[64,2,1024]{2,1,0:T(2,128)(2,1)} %reshape.136), calls=%async_computation | async-start | bytes 524288 | tf_op jit(solution)/shard_map/all_to_all | solution.py:22
  71.5 9.3 %all-to-all-done = bf16[64,2,1024]{2,1,0:T(2,128)(2,1)} async-done(((bf16[64,2,1024]{2,1,0:T(2,128)(2,1)}), bf16[64,2,1024]{2,1,0:T(2,128)(2,1)}, u32[]{:S(2)}, u32[]{:S(2)}) %all-to-all-start) | async-done | bytes 262176 | tf_op jit(solution)/shard_map/all_to_all | solution.py:22
  80.8 2.8 reshape.137
  83.6 3.2 bitcast_reduce_fusion.2
  88.6 4.5 add_bitcast_fusion
  93.3 3.0 copy.116
  96.3 6.2 %all-to-all-start.7 = ((f32[2,128,2,1024]{3,2,0,1:T(2,128)}), f32[2,128,2,1024]{3,2,0,1:T(2,128)S(1)}, u32[]{:S(2)}, u32[]{:S(2)}) async-start(f32[2,128,2,1024]{3,2,0,1:T(2,128)} %copy.116), calls=%async_computation.7 | async-start | bytes 4194304 | tf_op jit(solution)/shard_map/all_to_all | solution.py:32
  103.9 2.9 copy.100
  106.8 46.6 %all-to-all-done.7 = f32[2,128,2,1024]{3,2,0,1:T(2,128)S(1)} async-done(((f32[2,128,2,1024]{3,2,0,1:T(2,128)}), f32[2,128,2,1024]{3,2,0,1:T(2,128)S(1)}, u32[]{:S(2)}, u32[]{:S(2)}) %all-to-all-start.7) | async-done | bytes 2097184 | tf_op jit(solution)/shard_map/all_to_all | solution.py:32
  153.4 5.1 all-to-all-start.3
  160.0 3.0 copy.93
  162.9 26.1 %all-to-all-done.3 = f32[2,128,2,1024]{3,2,0,1:T(2,128)} async-done(((f32[2,128,2,1024]{3,2,0,1:T(2,128)}), f32[2,128,2,1024]{3,2,0,1:T(2,128)}, u32[]{:S(2)}, u32[]{:S(2)}) %all-to-all-start.3) | async-done | bytes 2097184 | tf_op jit(solution)/shard_map/all_to_all | solution.py:32
  189.0 25.6 %all-to-all-start.1 = ((f32[2,128,2,1024]{3,2,0,1:T(2,128)}), f32[2,128,2,1024]{3,2,0,1:T(2,128)}, u32[]{:S(2)}, u32[]{:S(2)}) async-start(f32[2,128,2,1024]{3,2,0,1:T(2,128)} %copy.93), calls=%async_computation.1 | async-start | bytes 4194304 | tf_op jit(solution)/shard_map/all_to_all | solution.py:32
  218.9 3.2 copy.156
  226.1 2.4 fusion.90
  228.5 2.3 fusion.88
  233.3 2.2 convolution_add_fusion.2
  235.5 2.2 convolution_add_fusion.4
  237.7 2.3 convolution_subtract_fusion.4
  240.0 25.5 %all-to-all-done.1 = f32[2,128,2,1024]{3,2,0,1:T(2,128)} async-done(((f32[2,128,2,1024]{3,2,0,1:T(2,128)}), f32[2,128,2,1024]{3,2,0,1:T(2,128)}, u32[]{:S(2)}, u32[]{:S(2)}) %all-to-all-start.1) | async-done | bytes 2097184 | tf_op jit(solution)/shard_map/all_to_all | solution.py:32
  265.5 3.2 copy.157
  276.5 2.8 multiply_add_fusion
  286.1 4.2 copy.127
  290.3 5.1 all-to-all-start.10
  301.8 4.2 copy.108
  306.0 19.8 %all-to-all-done.10 = f32[2,2,128,1024]{3,1,0,2:T(2,128)} async-done(((f32[2,2,128,1024]{3,1,0,2:T(2,128)}), f32[2,2,128,1024]{3,1,0,2:T(2,128)}, u32[]{:S(2)}, u32[]{:S(2)}) %all-to-all-start.10) | async-done | bytes 2097184 | tf_op jit(solution)/shard_map/all_to_all | solution.py:57
  325.9 26.0 %all-to-all-start.4 = ((f32[2,2,128,1024]{3,1,0,2:T(2,128)}), f32[2,2,128,1024]{3,1,0,2:T(2,128)}, u32[]{:S(2)}, u32[]{:S(2)}) async-start(f32[2,2,128,1024]{3,1,0,2:T(2,128)} %copy.108), calls=%async_computation.4 | async-start | bytes 4194304 | tf_op jit(solution)/shard_map/all_to_all | solution.py:57
  356.9 2.5 copy.122
  359.4 43.2 %all-to-all-done.4 = f32[2,2,128,1024]{3,1,0,2:T(2,128)} async-done(((f32[2,2,128,1024]{3,1,0,2:T(2,128)}), f32[2,2,128,1024]{3,1,0,2:T(2,128)}, u32[]{:S(2)}, u32[]{:S(2)}) %all-to-all-start.4) | async-done | bytes 2097184 | tf_op jit(solution)/shard_map/all_to_all | solution.py:57
  402.6 5.1 all-to-all-start.8
  407.7 2.3 copy.128
  417.9 20.2 %all-to-all-done.8 = f32[2,2,128,1024]{3,1,0,2:T(2,128)} async-done(((f32[2,2,128,1024]{3,1,0,2:T(2,128)}), f32[2,2,128,1024]{3,1,0,2:T(2,128)}, u32[]{:S(2)}, u32[]{:S(2)}) %all-to-all-start.8) | async-done | bytes 2097184 | tf_op jit(solution)/shard_map/all_to_all | solution.py:57
  438.2 25.8 %all-to-all-start.11 = ((f32[64,2,1024]{2,1,0:T(2,128)}), f32[64,2,1024]{2,1,0:T(2,128)}, u32[]{:S(2)}, u32[]{:S(2)}) async-start(f32[64,2,1024]{2,1,0:T(2,128)} %copy.131), calls=%async_computation.11 | async-start | bytes 1048576 | tf_op jit(solution)/shard_map/all_to_all | solution.py:64
  464.0 2.3 copy.109
  474.1 7.1 %all-to-all-done.11 = f32[64,2,1024]{2,1,0:T(2,128)} async-done(((f32[64,2,1024]{2,1,0:T(2,128)}), f32[64,2,1024]{2,1,0:T(2,128)}, u32[]{:S(2)}, u32[]{:S(2)}) %all-to-all-start.11) | async-done | bytes 524320 | tf_op jit(solution)/shard_map/all_to_all | solution.py:64
  481.2 8.1 %all-to-all-start.5 = ((f32[64,2,1024]{2,1,0:T(2,128)}), f32[64,2,1024]{2,1,0:T(2,128)}, u32[]{:S(2)}, u32[]{:S(2)}) async-start(f32[64,2,1024]{2,1,0:T(2,128)} %copy.112), calls=%async_computation.5 | async-start | bytes 1048576 | tf_op jit(solution)/shard_map/all_to_all | solution.py:64
  489.4 2.3 copy.123
  499.6 6.9 %all-to-all-done.5 = f32[64,2,1024]{2,1,0:T(2,128)} async-done(((f32[64,2,1024]{2,1,0:T(2,128)}), f32[64,2,1024]{2,1,0:T(2,128)}, u32[]{:S(2)}, u32[]{:S(2)}) %all-to-all-start.5) | async-done | bytes 524320 | tf_op jit(solution)/shard_map/all_to_all | solution.py:64
  506.4 7.5 %all-to-all-start.9 = ((f32[64,2,1024]{2,1,0:T(2,128)}), f32[64,2,1024]{2,1,0:T(2,128)S(1)}, u32[]{:S(2)}, u32[]{:S(2)}) async-start(f32[64,2,1024]{2,1,0:T(2,128)} %copy.126), calls=%async_computation.9 | async-start | bytes 1048576 | tf_op jit(solution)/shard_map/all_to_all | solution.py:64
  514.0 2.2 reshape.128
  518.0 13.3 %all-to-all-done.9 = f32[64,2,1024]{2,1,0:T(2,128)S(1)} async-done(((f32[64,2,1024]{2,1,0:T(2,128)}), f32[64,2,1024]{2,1,0:T(2,128)S(1)}, u32[]{:S(2)}, u32[]{:S(2)}) %all-to-all-start.9) | async-done | bytes 524320 | tf_op jit(solution)/shard_map/all_to_all | solution.py:64
  533.0 13.0 %reduce-scatter.2.cloned.1.call-done = f32[128,256]{1,0:T(8,128)} async-done(((f32[128,1024]{1,0:T(8,128)}), f32[128,256]{1,0:T(8,128)}) %reduce-scatter.2.cloned.1.call-update) | async-done | bytes 131088 | tf_op jit(solution)/shard_map/reduce_scatter | solution.py:101
  (119 shorter events, 84.7 us)
Async XLA Ops:
  7.2 20.6 %copy-start.8 = (f32[128,1024]{1,0:T(8,128)S(1)}, f32[128,1024]{1,0:T(8,128)}, u32[]{:S(2)}) copy-start(f32[128,1024]{1,0:T(8,128)} %param.7) | copy-start | bytes 1572868
  7.2 20.6 %copy-start.11 = (bf16[128,1024]{1,0:T(8,128)(2,1)S(1)}, bf16[128,1024]{1,0:T(8,128)(2,1)}, u32[]{:S(2)}) copy-start(bf16[128,1024]{1,0:T(8,128)(2,1)} %param.6) | copy-start | bytes 786436
  11.3 19.9 %copy-start.13 = (bf16[128,1024]{1,0:T(8,128)(2,1)S(1)}, bf16[128,1024]{1,0:T(8,128)(2,1)}, u32[]{:S(2)}) copy-start(bf16[128,1024]{1,0:T(8,128)(2,1)} %param.8) | copy-start | bytes 786436
  12.1 29.4 %all-to-all-start.6 = ((bf16[64,2,1024]{2,1,0:T(2,128)(2,1)}), bf16[64,2,1024]{2,1,0:T(2,128)(2,1)S(1)}, u32[]{:S(2)}, u32[]{:S(2)}) async-start(bf16[64,2,1024]{2,1,0:T(2,128)(2,1)} %reshape.140), calls=%async_computation.6 | async-start | bytes 524288 | tf_op jit(solution)/shard_map/all_to_all | solution.py:22
  41.5 19.8 %all-to-all-start.2 = ((bf16[64,2,1024]{2,1,0:T(2,128)(2,1)}), bf16[64,2,1024]{2,1,0:T(2,128)(2,1)S(1)}, u32[]{:S(2)}, u32[]{:S(2)}) async-start(bf16[64,2,1024]{2,1,0:T(2,128)(2,1)} %reshape.138), calls=%async_computation.2 | async-start | bytes 524288 | tf_op jit(solution)/shard_map/all_to_all | solution.py:22
  61.3 19.5 %all-to-all-start = ((bf16[64,2,1024]{2,1,0:T(2,128)(2,1)}), bf16[64,2,1024]{2,1,0:T(2,128)(2,1)}, u32[]{:S(2)}, u32[]{:S(2)}) async-start(bf16[64,2,1024]{2,1,0:T(2,128)(2,1)} %reshape.136), calls=%async_computation | async-start | bytes 524288 | tf_op jit(solution)/shard_map/all_to_all | solution.py:22
  96.3 6.2 %copy-start.3 = (f32[1,128,2,1024]{3,1,2,0:T(8,128)S(1)}, f32[1,128,2,1024]{3,1,2,0:T(8,128)}, u32[]{:S(2)}) copy-start(f32[1,128,2,1024]{3,1,2,0:T(8,128)} %get-tuple-element.33) | copy-start | bytes 3145732
  96.3 57.1 %all-to-all-start.7 = ((f32[2,128,2,1024]{3,2,0,1:T(2,128)}), f32[2,128,2,1024]{3,2,0,1:T(2,128)S(1)}, u32[]{:S(2)}, u32[]{:S(2)}) async-start(f32[2,128,2,1024]{3,2,0,1:T(2,128)} %copy.116), calls=%async_computation.7 | async-start | bytes 4194304 | tf_op jit(solution)/shard_map/all_to_all | solution.py:32
  106.8 51.7 %copy-start.2 = (f32[1,128,2,1024]{3,1,2,0:T(8,128)S(1)}, f32[1,128,2,1024]{3,1,2,0:T(8,128)}, u32[]{:S(2)}) copy-start(f32[1,128,2,1024]{3,1,2,0:T(8,128)} %get-tuple-element.35) | copy-start | bytes 3145732
  153.4 35.6 %all-to-all-start.3 = ((f32[2,128,2,1024]{3,2,0,1:T(2,128)}), f32[2,128,2,1024]{3,2,0,1:T(2,128)}, u32[]{:S(2)}, u32[]{:S(2)}) async-start(f32[2,128,2,1024]{3,2,0,1:T(2,128)} %copy.100), calls=%async_computation.3 | async-start | bytes 4194304 | tf_op jit(solution)/shard_map/all_to_all | solution.py:32
  189.0 76.5 %all-to-all-start.1 = ((f32[2,128,2,1024]{3,2,0,1:T(2,128)}), f32[2,128,2,1024]{3,2,0,1:T(2,128)}, u32[]{:S(2)}, u32[]{:S(2)}) async-start(f32[2,128,2,1024]{3,2,0,1:T(2,128)} %copy.93), calls=%async_computation.1 | async-start | bytes 4194304 | tf_op jit(solution)/shard_map/all_to_all | solution.py:32
  273.3 2.5 copy-start.6
  273.3 2.5 copy-start.7
  274.5 1.3 copy-start.1
  274.6 1.6 copy-start.4
  274.6 1.9 copy-start.5
  290.3 35.6 %all-to-all-start.10 = ((f32[2,2,128,1024]{3,1,0,2:T(2,128)}), f32[2,2,128,1024]{3,1,0,2:T(2,128)}, u32[]{:S(2)}, u32[]{:S(2)}) async-start(f32[2,2,128,1024]{3,1,0,2:T(2,128)} %copy.127), calls=%async_computation.10 | async-start | bytes 4194304 | tf_op jit(solution)/shard_map/all_to_all | solution.py:57
  295.4 1.2 copy-start
  325.9 76.7 %all-to-all-start.4 = ((f32[2,2,128,1024]{3,1,0,2:T(2,128)}), f32[2,2,128,1024]{3,1,0,2:T(2,128)}, u32[]{:S(2)}, u32[]{:S(2)}) async-start(f32[2,2,128,1024]{3,1,0,2:T(2,128)} %copy.108), calls=%async_computation.4 | async-start | bytes 4194304 | tf_op jit(solution)/shard_map/all_to_all | solution.py:57
  402.6 35.6 %all-to-all-start.8 = ((f32[2,2,128,1024]{3,1,0,2:T(2,128)}), f32[2,2,128,1024]{3,1,0,2:T(2,128)}, u32[]{:S(2)}, u32[]{:S(2)}) async-start(f32[2,2,128,1024]{3,1,0,2:T(2,128)} %copy.122), calls=%async_computation.8 | async-start | bytes 4194304 | tf_op jit(solution)/shard_map/all_to_all | solution.py:57
  438.2 43.0 %all-to-all-start.11 = ((f32[64,2,1024]{2,1,0:T(2,128)}), f32[64,2,1024]{2,1,0:T(2,128)}, u32[]{:S(2)}, u32[]{:S(2)}) async-start(f32[64,2,1024]{2,1,0:T(2,128)} %copy.131), calls=%async_computation.11 | async-start | bytes 1048576 | tf_op jit(solution)/shard_map/all_to_all | solution.py:64
  481.2 25.2 %all-to-all-start.5 = ((f32[64,2,1024]{2,1,0:T(2,128)}), f32[64,2,1024]{2,1,0:T(2,128)}, u32[]{:S(2)}, u32[]{:S(2)}) async-start(f32[64,2,1024]{2,1,0:T(2,128)} %copy.112), calls=%async_computation.5 | async-start | bytes 1048576 | tf_op jit(solution)/shard_map/all_to_all | solution.py:64
  506.4 24.9 %all-to-all-start.9 = ((f32[64,2,1024]{2,1,0:T(2,128)}), f32[64,2,1024]{2,1,0:T(2,128)S(1)}, u32[]{:S(2)}, u32[]{:S(2)}) async-start(f32[64,2,1024]{2,1,0:T(2,128)} %copy.126), calls=%async_computation.9 | async-start | bytes 1048576 | tf_op jit(solution)/shard_map/all_to_all | solution.py:64
  514.0 32.1 %reduce-scatter.2.cloned.1.call-start = ((), (), s32[]{:S(2)}) async-start(), calls=%async_computation.13 | async-start | bytes 655360 | tf_op jit(solution)/shard_map/reduce_scatter | solution.py:101
  516.2 15.7 %copy-start.9 = (f32[128,1024]{1,0:T(8,128)S(1)}, f32[128,1024]{1,0:T(8,128)}, u32[]{:S(2)}) copy-start(f32[128,1024]{1,0:T(8,128)} %param.7) | copy-start | bytes 1572868
  516.2 15.7 %copy-start.10 = (bf16[128,1024]{1,0:T(8,128)(2,1)S(1)}, bf16[128,1024]{1,0:T(8,128)(2,1)}, u32[]{:S(2)}) copy-start(bf16[128,1024]{1,0:T(8,128)(2,1)} %param.5) | copy-start | bytes 786436
  516.2 15.7 %copy-start.12 = (bf16[128,1024]{1,0:T(8,128)(2,1)S(1)}, bf16[128,1024]{1,0:T(8,128)(2,1)}, u32[]{:S(2)}) copy-start(bf16[128,1024]{1,0:T(8,128)(2,1)} %param.6) | copy-start | bytes 786436
  516.3 15.7 %copy-start.14 = (f32[1024]{0:T(1024)S(1)}, f32[1024]{0:T(1024)}, u32[]{:S(2)}) copy-start(f32[1024]{0:T(1024)} %param.9) | copy-start | bytes 12292
Sparse Core Ops, SparseCore 0:
  517.3 28.6 reduce-scatter.1
where the time goes:
time: 566 us; the launch traced here: 555 us
  waiting for transfers between devices  248 us (44%)
  starting transfers between devices  142 us (25%)
  local copies, waits for them, and re-layouts  80.5 us (14%)
  matrix products  51.5 us (9%)
  other arithmetic  17.3 us (3%)
  between operations  15.3 us (3%)
    all_to_all x3, waiting for transfers between devices, forward_spectrum(): lax.all_to_all(stacked, 'seq', split_axis=1, concat_axis=2, tiled=True)  98.2 us
    all_to_all x3, waiting for transfers between devices, inverse_signal(): lax.all_to_all(stacked, 'seq', split_axis=2, concat_axis=1, tiled=True)  83.3 us
    all_to_all x3, starting transfers between devices, inverse_signal(): lax.all_to_all(blocks, 'seq', split_axis=0, concat_axis=1, tiled=True)  41.4 us
    all_to_all x3, starting transfers between devices, forward_spectrum(): lax.all_to_all(stacked, 'seq', split_axis=1, concat_axis=2, tiled=True)  36.9 us
    all_to_all x3, starting transfers between devices, inverse_signal(): lax.all_to_all(stacked, 'seq', split_axis=2, concat_axis=1, tiled=True)  36.2 us
    all_to_all x3, starting transfers between devices, forward_spectrum(): lax.all_to_all(outgoing, 'seq', split_axis=1, concat_axis=0, tiled=True)  27.4 us
    all_to_all x3, waiting for transfers between devices, inverse_signal(): lax.all_to_all(blocks, 'seq', split_axis=0, concat_axis=1, tiled=True)  27.2 us
    all_to_all x3, waiting for transfers between devices, forward_spectrum(): lax.all_to_all(outgoing, 'seq', split_axis=1, concat_axis=0, tiled=True)  26.6 us
  transfers between devices with their start and end apart: 13, of which 13 were waited for; matrix products, arithmetic and copies ran while one was open for 18% of the time, Pallas kernels for 0%

commit v1 on v0

v1 whole, which is shorter than its diff:
```python
import math

import jax
import jax.numpy as jnp
import numpy as np
from jax import lax
from jax.experimental import pallas as pl
from jax.experimental.pallas import tpu as pltpu
from jax.sharding import PartitionSpec as P

F32 = jnp.float32
BF16 = jnp.bfloat16
VMEM = pl.BlockSpec(memory_space=pltpu.VMEM)


def split_pair(table):
    high = table.astype(np.float32).astype(jnp.bfloat16)
    low = (table - high.astype(np.float64)).astype(np.float32).astype(jnp.bfloat16)
    return high, low


def tables(blocks, rows):
    period = 2 * blocks * rows
    scale = 2.0 / period / math.sqrt(blocks * rows)
    half = np.arange(blocks) + 0.5
    block_angle = 2.0 * np.pi / (2 * blocks) * np.outer(half, np.arange(blocks))
    enter = np.concatenate([np.cos(block_angle), -np.sin(block_angle)], axis=0)
    leave = np.concatenate([np.cos(block_angle), -np.sin(block_angle)], axis=0).T * scale
    turn = 2.0 * np.pi / period * np.outer(half, np.arange(rows))
    row_angle = 2.0 * np.pi / rows * np.outer(np.arange(rows), np.arange(rows))
    row_cos, row_sin = np.cos(row_angle), np.sin(row_angle)
    forward = np.block([[row_cos, -row_sin], [row_sin, row_cos]])
    inverse = np.block([[row_cos, row_sin], [-row_sin, row_cos]])
    enter_pair = np.concatenate(split_pair(enter), axis=0)
    leave_high, leave_low = split_pair(leave)
    leave_pair = np.concatenate([leave_high, leave_low], axis=0)
    return (
        enter_pair,
        leave_pair,
        *split_pair(forward),
        *split_pair(inverse),
        np.cos(turn).astype(np.float32),
        np.sin(turn).astype(np.float32),
    )


def split_value(x):
    high = x.astype(BF16)
    return high, (x - high.astype(F32)).astype(BF16)


def dot(a, b):
    return jnp.dot(a, b, preferred_element_type=F32)


def dot_wide(x, high, low):
    x_high, x_low = split_value(x)
    return dot(x_high, high) + (dot(x_low, high) + dot(x_high, low))


def pack_kernel(values_ref, gates_ref, grad_ref, filter_ref, out_ref):
    group = out_ref.shape[1] // 3
    parts = (
        values_ref[...].astype(F32),
        (grad_ref[...] * gates_ref[...].astype(F32)).astype(BF16).astype(F32),
        filter_ref[...].astype(F32),
    )
    for a, part in enumerate(parts):
        turned = part.T.astype(BF16)
        out_ref[:, a * group : (a + 1) * group, :] = turned.reshape(-1, group, part.shape[0])


def spectra_kernel(
    in_ref, enter_ref, leave_ref, fwd_h, fwd_l, inv_h, inv_l, cos_ref, sin_ref, out_ref, wide, result
):
    blocks, rows = in_ref.shape[0], in_ref.shape[2]
    group = in_ref.shape[1] // 3
    step = 4
    for a in range(3):
        part = in_ref[:, a * group : (a + 1) * group, :]
        wide[a] = part.astype(F32).reshape(blocks * group, rows)
    cos_t, sin_t = cos_ref[...], sin_ref[...]

    def spectrum(a, c0):
        cols = [wide[a, pl.ds(c0 + c, blocks, stride=group), :] for c in range(step)]
        mixed = dot(enter_ref[...], jnp.concatenate(cols, axis=1).astype(BF16))
        mixed = mixed[: 2 * blocks] + mixed[2 * blocks :]
        turned = []
        for c in range(step):
            re = mixed[:blocks, c * rows : (c + 1) * rows]
            im = mixed[blocks:, c * rows : (c + 1) * rows]
            turned.append(
                jnp.concatenate([re * cos_t + im * sin_t, im * cos_t - re * sin_t], axis=1)
            )
        full = dot_wide(jnp.concatenate(turned, axis=0), fwd_h[...], fwd_l[...])
        return full[:, :rows], full[:, rows:]

    def signal(a, c0, re, im):
        full = dot_wide(jnp.concatenate([re, im], axis=1), inv_h[...], inv_l[...])
        cols = []
        for c in range(step):
            re = full[c * blocks : (c + 1) * blocks, :rows]
            im = full[c * blocks : (c + 1) * blocks, rows:]
            cols.append(
                jnp.concatenate([re * cos_t - im * sin_t, re * sin_t + im * cos_t], axis=0)
            )
        high, low = split_value(jnp.concatenate(cols, axis=1))
        pair = dot(leave_ref[...], high)
        mixed = pair[:blocks] + (pair[blocks:] + dot(leave_ref[:blocks, :], low))
        for c in range(step):
            result[a, pl.ds(c0 + c, blocks, stride=group), :] = mixed[:, c * rows : (c + 1) * rows]

    for c0 in range(0, group, step):
        v_re, v_im = spectrum(0, c0)
        g_re, g_im = spectrum(1, c0)
        h_re, h_im = spectrum(2, c0)
        signal(0, c0, h_re * v_re - h_im * v_im, h_re * v_im + h_im * v_re)
        signal(1, c0, h_re * g_re + h_im * g_im, h_re * g_im - h_im * g_re)
        signal(2, c0, v_re * g_re + v_im * g_im, v_re * g_im - v_im * g_re)
    for a in range(3):
        out_ref[:, a * group : (a + 1) * group, :] = (
            result[a].astype(BF16).reshape(blocks, group, rows)
        )


def finish_kernel(values_ref, gates_ref, grad_ref, skip_ref, in_ref, value_out, gate_out):
    group = in_ref.shape[1] // 3
    rows = in_ref.shape[2]

    def part(a):
        piece = in_ref[:, a * group : (a + 1) * group, :].astype(F32)
        return piece.reshape(-1, rows).T

    grad = grad_ref[...]
    skip = skip_ref[...]
    mixed = part(0) + skip * values_ref[...].astype(F32)
    gate_out[...] = (grad * mixed).astype(BF16)
    gate_term = (grad * gates_ref[...].astype(F32)).astype(BF16).astype(F32)
    value_out[...] = (part(1) + skip * gate_term).astype(BF16)


def sum_kernel(*refs):
    out_ref = refs[-1]
    rows = out_ref.shape[0]
    total = refs[0][...].astype(F32)
    for ref in refs[1:-1]:
        total = total + ref[...].astype(F32)
    out_ref[...] = total.reshape(-1, rows).T


def local(values, gates, grad_out, filter_raw, skip_gain):
    rows, width = values.shape
    blocks = lax.axis_size("seq")
    copies = lax.axis_size("chan")
    group = width // blocks
    rank = lax.axis_index("chan")
    limit = pltpu.CompilerParams(vmem_limit_bytes=48 * 1024 * 1024)
    packed = jax.ShapeDtypeStruct((blocks, 3 * group, rows), BF16)
    sent = pl.pallas_call(
        pack_kernel, out_shape=packed, in_specs=[VMEM] * 4, out_specs=VMEM, compiler_params=limit
    )(values, gates, grad_out, filter_raw)
    held = lax.all_to_all(sent, "seq", split_axis=0, concat_axis=0, tiled=True)
    consts = tables(blocks, rows)
    done = pl.pallas_call(
        spectra_kernel,
        out_shape=packed,
        in_specs=[VMEM] * (1 + len(consts)),
        out_specs=VMEM,
        scratch_shapes=[
            pltpu.VMEM((3, blocks * group, rows), F32),
            pltpu.VMEM((3, blocks * group, rows), F32),
        ],
        compiler_params=limit,
    )(held, *consts)
    back = lax.all_to_all(done, "seq", split_axis=0, concat_axis=0, tiled=True)
    terms = back[:, 2 * group :, :]
    share = blocks // copies
    pieces = [
        lax.dynamic_slice_in_dim(terms, lax.rem(rank + d, copies) * share, share, 0)
        for d in range(copies)
    ]
    for d in range(1, copies):
        pieces[d] = lax.ppermute(
            pieces[d], "chan", [(src, (src + d) % copies) for src in range(copies)]
        )
    shape = jax.ShapeDtypeStruct((rows, width), BF16)
    value_grad, gate_grad = pl.pallas_call(
        finish_kernel,
        out_shape=(shape, shape),
        in_specs=[VMEM] * 5,
        out_specs=(VMEM, VMEM),
        compiler_params=limit,
    )(values, gates, grad_out, skip_gain[None, :], back)
    filter_grad = pl.pallas_call(
        sum_kernel,
        out_shape=jax.ShapeDtypeStruct((rows, width // copies), F32),
        in_specs=[VMEM] * copies,
        out_specs=VMEM,
        compiler_params=limit,
    )(*pieces)
    return (value_grad, gate_grad, filter_grad)


def solution(mesh):
    in_specs = (P("seq", "chan"), P("seq", "chan"), P("seq", "chan"), P("seq", None), P("chan"))
    out_specs = (P("seq", "chan"), P("seq", "chan"), P("seq", "chan"))
    return jax.shard_map(local, mesh=mesh, in_specs=in_specs, out_specs=out_specs, check_vma=False)
```

time: 566 us -> 95.7 us (0.17); the launches traced: 555 us -> 95.2 us
  waiting for transfers between devices: 248 us -> 24.3 us
  starting transfers between devices: 142 us -> 16.9 us
  local copies, waits for them, and re-layouts: 80.5 us -> 4.01 us
  matrix products: 51.5 us -> 0 us
  blocking collectives: 0 us -> 37.6 us
  other arithmetic: 17.3 us -> 0 us
  between operations: 15.3 us -> 0.84 us
  Pallas kernels: 0 us -> 11.5 us
    all_to_all x12 -> x1, waiting for transfers between devices: 235 us -> 22.9 us  [local(): back = lax.all_to_all(done, 'seq', split_axis=0, concat_axis=0, tiled=True)]
    all_to_all x12 -> x1, starting transfers between devices: 142 us -> 7.54 us  [local(): back = lax.all_to_all(done, 'seq', split_axis=0, concat_axis=0, tiled=True)]
    dot_general x36 -> x0, matrix products: 51.5 us -> none  [the longest x3 7.03 us: forward_spectrum(): real_part = jnp.einsum('ka,ajc->kjc', block_cos, columns, precision=EXACT)]
    all_to_all x0 -> x1, blocking collectives: none -> 37.6 us  [local(): held = lax.all_to_all(sent, 'seq', split_axis=0, concat_axis=0, tiled=True)]
    all_to_all x12 -> x0, local copies, waits for them, and re-layouts: 22.5 us -> none  [the longest x3 8.04 us: forward_spectrum(): lax.all_to_all(stacked, 'seq', split_axis=1, concat_axis=2, tiled=True)]
    another operation x6 -> x0, local copies, waits for them, and re-layouts: 19.7 us -> none  [the longest x3 10.9 us: inverse_signal(): stacked = jnp.stack([real_rows, imag_rows])]
    slice x12 -> x1, local copies, waits for them, and re-layouts: 13.1 us -> 0.02 us  [local(): terms = back[:, 2 * group:, :]]
    reduce_scatter x1 -> x0, waiting for transfers between devices: 13 us -> none  [local(): lax.psum_scatter(terms, 'chan', scatter_dimension=1, tiled=True) * scale]
  transfers between devices with their start and end apart: 13 -> 4, of which waited for: 13 -> 2; matrix products, arithmetic and copies ran while one was open for 18% -> 0% of each run, Pallas kernels for 0% -> 1%
where the time goes in v1:
time: 95.7 us; the launch traced here: 95.2 us
  blocking collectives  37.6 us (39%)
  waiting for transfers between devices  24.3 us (25%)
  starting transfers between devices  16.9 us (18%)
  Pallas kernels  11.5 us (12%)
  local copies, waits for them, and re-layouts  4.01 us (4%)
    all_to_all x1, blocking collectives, local(): held = lax.all_to_all(sent, 'seq', split_axis=0, concat_axis=0, tiled=True)  37.6 us
    all_to_all x1, waiting for transfers between devices, local(): back = lax.all_to_all(done, 'seq', split_axis=0, concat_axis=0, tiled=True)  22.9 us
    pallas_call x1, Pallas kernels, local(): pl.pallas_call(spectra_kernel, out_shape=packed, in_specs=[VMEM] * (1 + l...  9.54 us
    ppermute x3, starting transfers between devices, local(): lax.ppermute(pieces[d], 'chan', [(src, (src + d) % copies) for src in ran...  9.34 us
    all_to_all x1, starting transfers between devices, local(): back = lax.all_to_all(done, 'seq', split_axis=0, concat_axis=0, tiled=True)  7.54 us
    unnamed x32, local copies, waits for them, and re-layouts  3.97 us
  transfers between devices with their start and end apart: 4, of which 2 were waited for; matrix products, arithmetic and copies ran while one was open for 0% of the time, Pallas kernels for 1%

profile of v1, /device:TPU:1, one launch (start us, length us, event | category | flops | bytes accessed | tf_op | source)
XLA Modules:
  0.0 95.2 jit_solution(4456997365883469758)
XLA Ops:
  0.6 0.0 copy-start
  0.6 1.0 %copy-done = f32[128,1024]{1,0:T(8,128)S(1)} copy-done((f32[128,1024]{1,0:T(8,128)S(1)}, f32[128,1024]{1,0:T(8,128)}, u32[]{:S(2)}) %copy-start) | copy-done | bytes 524312
  1.7 0.0 copy-start.2
  1.7 0.9 copy-done.2
  2.6 0.0 copy-start.4
  2.6 0.9 copy-done.4
  3.6 0.0 copy-start.6
  3.6 0.9 copy-done.6
  4.5 0.3 shard_map.148
  4.8 0.0 copy-start.7
  4.8 0.0 copy-start.8
  4.8 0.0 copy-start.9
  4.8 0.0 copy-start.10
  4.9 0.0 copy-start.11
  4.9 0.0 copy-start.12
  4.9 0.0 copy-start.13
  4.9 0.0 copy-start.14
  4.9 37.6 %all_to_all.10.in_ref = bf16[64,48,128]{2,1,0:T(8,128)(2,1)S(1)} all-to-all(bf16[64,48,128]{2,1,0:T(8,128)(2,1)S(1)} %shard_map.148), channel_id=1, replica_groups=mesh['seq'=64,'chan'=4] {'seq'}, dimensions={0} | all-to-all | bytes 1572864 | tf_op jit(solution)/shard_map/all_to_all | solution.py:162
  42.5 0.0 copy-done.7
  42.5 0.0 copy-done.8
  42.5 0.0 copy-done.9
  42.5 0.0 copy-done.10
  42.5 0.0 copy-done.11
  42.5 0.0 copy-done.12
  42.5 0.0 copy-done.13
  42.6 0.0 copy-done.14
  42.6 9.5 %shard_map.149 = bf16[64,48,128]{2,1,0:T(8,128)(2,1)} custom-call(bf16[64,48,128]{2,1,0:T(8,128)(2,1)S(1)} %all_to_all.10.in_ref, bf16[256,64]{1,0:T(8,128)(2,1)S(1)} %copy-done.11, bf16[128,128]{1,0:T(8,128)(2,1)S(1)} %copy-done.12, bf16[256,256]{1,0:T(8,128)(2,1)S(1)} %copy-done.7, bf16[256,256]{1,0:T(8,128)(2,1)S(1)} %copy-done.8, ...), custom_call_target="tpu_custom_call" | custom-call | tf_op jit(solution)/shard_map/pallas_call | solution.py:164
  52.1 7.5 %all-to-all-start.1 = ((bf16[64,48,128]{2,1,0:T(8,128)(2,1)}), bf16[64,48,128]{2,1,0:T(8,128)(2,1)S(1)}, u32[]{:S(2)}, u32[]{:S(2)}) async-start(bf16[64,48,128]{2,1,0:T(8,128)(2,1)} %shard_map.149), calls=%async_computation.1 | async-start | bytes 1572864 | tf_op jit(solution)/shard_map/all_to_all | solution.py:175
  59.7 0.0 copy-start.1
  59.7 22.9 %all-to-all-done.1.in_ref = bf16[64,48,128]{2,1,0:T(8,128)(2,1)S(1)} async-done(((bf16[64,48,128]{2,1,0:T(8,128)(2,1)}), bf16[64,48,128]{2,1,0:T(8,128)(2,1)S(1)}, u32[]{:S(2)}, u32[]{:S(2)}) %all-to-all-start.1) | async-done | bytes 786464 | tf_op jit(solution)/shard_map/all_to_all | solution.py:175
  82.6 0.0 copy-start.3
  82.6 0.0 copy-start.5
  82.7 0.0 copy-start.15
  82.7 6.6 %collective-permute-start = (bf16[16,16,128]{2,1,0:T(8,128)(2,1)S(1)}, bf16[16,16,128]{2,1,0:T(8,128)(2,1)S(1)}, u32[]{:S(2)}, u32[]{:S(2)}) collective-permute-start(bf16[16,16,128]{2,1,0:T(8,128)(2,1)S(1)} %get-tuple-element.9), channel_id=1, source_target_pairs={{0,1},{1,2},{2,3},{3,0},{4,5},{5,6},{6,7},{7,4},{8,9},{9,10},{10,1... | collective-permute-start | bytes 196616 | tf_op jit(solution)/shard_map/ppermute | solution.py:183
  89.3 0.5 collective-permute-start.1
  89.8 2.3 %collective-permute-start.2 = (bf16[16,16,128]{2,1,0:T(8,128)(2,1)S(1)}, bf16[16,16,128]{2,1,0:T(8,128)(2,1)S(1)}, u32[]{:S(2)}, u32[]{:S(2)}) collective-permute-start(bf16[16,16,128]{2,1,0:T(8,128)(2,1)S(1)} %get-tuple-element.7), channel_id=1, source_target_pairs={{0,3},{1,0},{2,1},{3,2},{4,7},{5,4},{6,5},{7,6},{8,11},{9,8},{10,9... | collective-permute-start | bytes 196616 | tf_op jit(solution)/shard_map/ppermute | solution.py:183
  92.0 0.0 copy-done.1
  92.1 0.0 copy-done.3
  92.1 0.0 copy-done.5
  92.1 0.0 copy-done.15
  92.1 1.0 %shard_map.150 = (bf16[128,1024]{1,0:T(8,128)(2,1)}, bf16[128,1024]{1,0:T(8,128)(2,1)}) custom-call(bf16[128,1024]{1,0:T(8,128)(2,1)S(1)} %copy-done.3, bf16[128,1024]{1,0:T(8,128)(2,1)S(1)} %copy-done.5, f32[128,1024]{1,0:T(8,128)S(1)} %copy-done.1, f32[1,1024]{1,0:T(1,128)S(1)} %bitcast.1, bf16[64,48,128]{2,1,0:T(8,128)(2,1)S(1)} %all-to-all-done.1.in_ref), custom_call_target="tpu_custom_call" | custom-call | tf_op jit(solution)/shard_map/pallas_call | solution.py:187
  93.0 0.0 collective-permute-done.refs_1_
  93.0 1.4 %collective-permute-done.1.refs_2_ = bf16[16,16,128]{2,1,0:T(8,128)(2,1)S(1)} collective-permute-done((bf16[16,16,128]{2,1,0:T(8,128)(2,1)S(1)}, bf16[16,16,128]{2,1,0:T(8,128)(2,1)S(1)}, u32[]{:S(2)}, u32[]{:S(2)}) %collective-permute-start.1) | collective-permute-done | bytes 65568 | tf_op jit(solution)/shard_map/ppermute | solution.py:183
  94.4 0.0 collective-permute-done.2.refs_3_
  94.4 0.8 shard_map.151
  (2 shorter events, 0.0 us)
Async XLA Ops:
  0.6 1.0 %copy-start = (f32[128,1024]{1,0:T(8,128)S(1)}, f32[128,1024]{1,0:T(8,128)}, u32[]{:S(2)}) copy-start(f32[128,1024]{1,0:T(8,128)} %grad_ref.3) | copy-start | bytes 1572868
  1.7 0.9 copy-start.2
  2.6 0.9 copy-start.4
  3.6 0.9 copy-start.6
  4.8 37.7 %copy-start.7 = (bf16[256,256]{1,0:T(8,128)(2,1)S(1)}, bf16[256,256]{1,0:T(8,128)(2,1)}, u32[]{:S(2)}) copy-start(bf16[256,256]{1,0:T(8,128)(2,1)} %constant.43.clone.fwd_h) | copy-start | bytes 393220
  4.8 37.7 %copy-start.8 = (bf16[256,256]{1,0:T(8,128)(2,1)S(1)}, bf16[256,256]{1,0:T(8,128)(2,1)}, u32[]{:S(2)}) copy-start(bf16[256,256]{1,0:T(8,128)(2,1)} %constant.44.clone.fwd_l) | copy-start | bytes 393220
  4.8 37.7 %copy-start.9 = (bf16[256,256]{1,0:T(8,128)(2,1)S(1)}, bf16[256,256]{1,0:T(8,128)(2,1)}, u32[]{:S(2)}) copy-start(bf16[256,256]{1,0:T(8,128)(2,1)} %constant.45.clone.inv_h) | copy-start | bytes 393220
  4.8 37.7 %copy-start.10 = (bf16[256,256]{1,0:T(8,128)(2,1)S(1)}, bf16[256,256]{1,0:T(8,128)(2,1)}, u32[]{:S(2)}) copy-start(bf16[256,256]{1,0:T(8,128)(2,1)} %constant.46.clone.inv_l) | copy-start | bytes 393220
  4.9 37.7 %copy-start.11 = (bf16[256,64]{1,0:T(8,128)(2,1)S(1)}, bf16[256,64]{1,0:T(8,128)(2,1)}, u32[]{:S(2)}) copy-start(bf16[256,64]{1,0:T(8,128)(2,1)} %constant.41.clone.enter_ref) | copy-start | bytes 98308
  4.9 37.7 %copy-start.12 = (bf16[128,128]{1,0:T(8,128)(2,1)S(1)}, bf16[128,128]{1,0:T(8,128)(2,1)}, u32[]{:S(2)}) copy-start(bf16[128,128]{1,0:T(8,128)(2,1)} %constant.42.clone.leave_ref) | copy-start | bytes 98308
  4.9 37.7 %copy-start.13 = (f32[64,128]{1,0:T(8,128)S(1)}, f32[64,128]{1,0:T(8,128)}, u32[]{:S(2)}) copy-start(f32[64,128]{1,0:T(8,128)} %constant.47.clone.cos_ref) | copy-start | bytes 98308
  4.9 37.7 %copy-start.14 = (f32[64,128]{1,0:T(8,128)S(1)}, f32[64,128]{1,0:T(8,128)}, u32[]{:S(2)}) copy-start(f32[64,128]{1,0:T(8,128)} %constant.48.clone.sin_ref) | copy-start | bytes 98308
  52.1 30.5 %all-to-all-start.1 = ((bf16[64,48,128]{2,1,0:T(8,128)(2,1)}), bf16[64,48,128]{2,1,0:T(8,128)(2,1)S(1)}, u32[]{:S(2)}, u32[]{:S(2)}) async-start(bf16[64,48,128]{2,1,0:T(8,128)(2,1)} %shard_map.149), calls=%async_computation.1 | async-start | bytes 1572864 | tf_op jit(solution)/shard_map/all_to_all | solution.py:175
  59.7 32.4 %copy-start.1 = (f32[128,1024]{1,0:T(8,128)S(1)}, f32[128,1024]{1,0:T(8,128)}, u32[]{:S(2)}) copy-start(f32[128,1024]{1,0:T(8,128)} %grad_ref.3) | copy-start | bytes 1572868
  82.6 9.4 %copy-start.3 = (bf16[128,1024]{1,0:T(8,128)(2,1)S(1)}, bf16[128,1024]{1,0:T(8,128)(2,1)}, u32[]{:S(2)}) copy-start(bf16[128,1024]{1,0:T(8,128)(2,1)} %values_ref.3) | copy-start | bytes 786436
  82.6 9.4 %copy-start.5 = (bf16[128,1024]{1,0:T(8,128)(2,1)S(1)}, bf16[128,1024]{1,0:T(8,128)(2,1)}, u32[]{:S(2)}) copy-start(bf16[128,1024]{1,0:T(8,128)(2,1)} %gates_ref.3) | copy-start | bytes 786436
  82.7 9.4 %copy-start.15 = (f32[1024]{0:T(1024)S(1)}, f32[1024]{0:T(1024)}, u32[]{:S(2)}) copy-start(f32[1024]{0:T(1024)} %param.17) | copy-start | bytes 12292
  82.7 10.3 %collective-permute-start = (bf16[16,16,128]{2,1,0:T(8,128)(2,1)S(1)}, bf16[16,16,128]{2,1,0:T(8,128)(2,1)S(1)}, u32[]{:S(2)}, u32[]{:S(2)}) collective-permute-start(bf16[16,16,128]{2,1,0:T(8,128)(2,1)S(1)} %get-tuple-element.9), channel_id=1, source_target_pairs={{0,1},{1,2},{2,3},{3,0},{4,5},{5,6},{6,7},{7,4},{8,9},{9,10},{10,1... | collective-permute-start | bytes 196616 | tf_op jit(solution)/shard_map/ppermute | solution.py:183
  89.3 5.1 %collective-permute-start.1 = (bf16[16,16,128]{2,1,0:T(8,128)(2,1)S(1)}, bf16[16,16,128]{2,1,0:T(8,128)(2,1)S(1)}, u32[]{:S(2)}, u32[]{:S(2)}) collective-permute-start(bf16[16,16,128]{2,1,0:T(8,128)(2,1)S(1)} %get-tuple-element.8), channel_id=1, source_target_pairs={{0,2},{1,3},{2,0},{3,1},{4,6},{5,7},{6,4},{7,5},{8,10},{9,11},{10,... | collective-permute-start | bytes 196616 | tf_op jit(solution)/shard_map/ppermute | solution.py:183
  89.8 4.6 %collective-permute-start.2 = (bf16[16,16,128]{2,1,0:T(8,128)(2,1)S(1)}, bf16[16,16,128]{2,1,0:T(8,128)(2,1)S(1)}, u32[]{:S(2)}, u32[]{:S(2)}) collective-permute-start(bf16[16,16,128]{2,1,0:T(8,128)(2,1)S(1)} %get-tuple-element.7), channel_id=1, source_target_pairs={{0,3},{1,0},{2,1},{3,2},{4,7},{5,4},{6,5},{7,6},{8,11},{9,8},{10,9... | collective-permute-start | bytes 196616 | tf_op jit(solution)/shard_map/ppermute | solution.py:183

commit v2 on v1

v2 whole, which is shorter than its diff:
```python
import math

import jax
import jax.numpy as jnp
import numpy as np
from jax import lax
from jax.experimental import pallas as pl
from jax.experimental.pallas import tpu as pltpu
from jax.sharding import PartitionSpec as P

F32 = jnp.float32
BF16 = jnp.bfloat16
VMEM = pl.BlockSpec(memory_space=pltpu.VMEM)
SHARES = 4
GROUP = 16
STEP = GROUP // SHARES
TAIL = 8
WIDE = True


def split_pair(table):
    high = table.astype(np.float32).astype(jnp.bfloat16)
    low = (table - high.astype(np.float64)).astype(np.float32).astype(jnp.bfloat16)
    return high, low


def tables(blocks, rows):
    period = 2 * blocks * rows
    scale = 2.0 / period / math.sqrt(blocks * rows)
    half = np.arange(blocks) + 0.5
    block_angle = 2.0 * np.pi / (2 * blocks) * np.outer(half, np.arange(blocks))
    enter = np.concatenate([np.cos(block_angle), -np.sin(block_angle)], axis=0)
    leave = np.concatenate([np.cos(block_angle), -np.sin(block_angle)], axis=0).T * scale
    turn = 2.0 * np.pi / period * np.outer(half, np.arange(rows))
    row_angle = 2.0 * np.pi / rows * np.outer(np.arange(rows), np.arange(rows))
    row_cos, row_sin = np.cos(row_angle), np.sin(row_angle)
    forward = np.block([[row_cos, -row_sin], [row_sin, row_cos]])
    inverse = np.block([[row_cos, row_sin], [-row_sin, row_cos]])
    enter_pair = np.concatenate(split_pair(enter), axis=0)
    leave_high, leave_low = split_pair(leave)
    leave_pair = np.concatenate([leave_high, leave_low], axis=0)
    if not WIDE:
        enter_pair = enter_pair[: 2 * blocks]
    return (
        enter_pair,
        leave_pair,
        *split_pair(forward),
        *split_pair(inverse),
        np.cos(turn).astype(np.float32),
        np.sin(turn).astype(np.float32),
    )


def split_value(x):
    high = x.astype(BF16)
    return high, (x - high.astype(F32)).astype(BF16)


def dot(a, b):
    return jnp.dot(a, b, preferred_element_type=F32)


def dot_wide(x, high, low):
    if not WIDE:
        return dot(x.astype(BF16), high)
    x_high, x_low = split_value(x)
    return dot(x_high, high) + (dot(x_low, high) + dot(x_high, low))


def pack_kernel(values_ref, gates_ref, grad_ref, filter_ref, out_ref, values, gates, grad, taps, flat, mixed, sems):
    group = out_ref.shape[1] // 3
    blocks = out_ref.shape[0]
    share = group // SHARES
    copies = [
        pltpu.make_async_copy(src, dst, sems.at[k])
        for k, (src, dst) in enumerate(
            ((values_ref, values), (filter_ref, taps), (gates_ref, gates), (grad_ref, grad))
        )
    ]
    for copy in copies:
        copy.start()

    def place(a, part):
        flat[a] = part.T
        for q in range(SHARES):
            for i in range(share):
                row = flat[a, pl.ds(q * share * blocks + i, blocks, stride=share), :]
                mixed[a, pl.ds(q * share + i, blocks, stride=group), :] = row
        turned = mixed[a].astype(BF16)
        out_ref[:, a * group : (a + 1) * group, :] = turned.reshape(blocks, group, -1)

    copies[0].wait()
    place(0, values[...].astype(F32))
    copies[1].wait()
    place(2, taps[...].astype(F32))
    copies[2].wait()
    copies[3].wait()
    place(1, (grad[...] * gates[...].astype(F32)).astype(BF16).astype(F32))


def spectrum(wide, a, c0, enter_ref, fwd_h, fwd_l, cos_t, sin_t):
    blocks, rows = cos_t.shape
    cols = [wide[a, pl.ds(c0 + c, blocks, stride=GROUP), :] for c in range(STEP)]
    mixed = dot(enter_ref[...], jnp.concatenate(cols, axis=1).astype(BF16))
    if enter_ref.shape[0] > 2 * blocks:
        mixed = mixed[: 2 * blocks] + mixed[2 * blocks :]
    turned = []
    for c in range(STEP):
        re = mixed[:blocks, c * rows : (c + 1) * rows]
        im = mixed[blocks:, c * rows : (c + 1) * rows]
        turned.append(jnp.concatenate([re * cos_t + im * sin_t, im * cos_t - re * sin_t], axis=1))
    return dot_wide(jnp.concatenate(turned, axis=0), fwd_h[...], fwd_l[...])


def signal(re, im, leave_ref, inv_h, inv_l, cos_t, sin_t):
    blocks, rows = cos_t.shape
    full = dot_wide(jnp.concatenate([re, im], axis=1), inv_h[...], inv_l[...])
    cols = []
    for c in range(STEP):
        re = full[c * blocks : (c + 1) * blocks, :rows]
        im = full[c * blocks : (c + 1) * blocks, rows:]
        cols.append(jnp.concatenate([re * cos_t - im * sin_t, re * sin_t + im * cos_t], axis=0))
    joined = jnp.concatenate(cols, axis=1)
    if not WIDE:
        return dot(leave_ref[:blocks, :], joined.astype(BF16))
    high, low = split_value(joined)
    pair = dot(leave_ref[...], high)
    return pair[:blocks] + (pair[blocks:] + dot(leave_ref[:blocks, :], low))


def conj_product(left, right):
    rows = left.shape[1] // 2
    l_re, l_im, r_re, r_im = left[:, :rows], left[:, rows:], right[:, :rows], right[:, rows:]
    return l_re * r_re + l_im * r_im, l_re * r_im - l_im * r_re


def plain_product(left, right):
    rows = left.shape[1] // 2
    l_re, l_im, r_re, r_im = left[:, :rows], left[:, rows:], right[:, :rows], right[:, rows:]
    return l_re * r_re - l_im * r_im, l_re * r_im + l_im * r_re


def chunk(ref, c0, blocks):
    return ref[pl.ds(c0 * blocks, STEP * blocks), :]


def terms_kernel(
    rank_ref, in_ref, enter_ref, leave_ref, fwd_h, fwd_l, inv_h, inv_l, cos_ref, sin_ref, *rest
):
    pieces, (v_ref, g_ref, wide) = rest[:SHARES], rest[SHARES:]
    blocks, rows = in_ref.shape[0], in_ref.shape[2]
    cos_t, sin_t = cos_ref[...], sin_ref[...]
    for a in range(2):
        part = in_ref[:, a * GROUP : (a + 1) * GROUP, :]
        wide[a] = part.astype(F32).reshape(blocks * GROUP, rows)
    for c0 in range(0, GROUP, STEP):
        for a, ref in enumerate((v_ref, g_ref)):
            ref[c0 * blocks : (c0 + STEP) * blocks, :] = spectrum(
                wide, a, c0, enter_ref, fwd_h, fwd_l, cos_t, sin_t
            )
    rank = rank_ref[0]
    for d in range(SHARES):
        start = pl.multiple_of(lax.rem(rank + d, SHARES) * (STEP * blocks), STEP * blocks)
        v = v_ref[pl.ds(start, STEP * blocks), :]
        g = g_ref[pl.ds(start, STEP * blocks), :]
        out = signal(*conj_product(v, g), leave_ref, inv_h, inv_l, cos_t, sin_t)
        for c in range(STEP):
            pieces[d][c] = out[:, c * rows : (c + 1) * rows].astype(BF16)


def conv_kernel(
    in_ref, v_ref, enter_ref, leave_ref, fwd_h, fwd_l, inv_h, inv_l, cos_ref, sin_ref, out_ref, h_ref, wide, result
):
    blocks, rows = in_ref.shape[0], in_ref.shape[2]
    cos_t, sin_t = cos_ref[...], sin_ref[...]
    wide[0] = in_ref[:, 2 * GROUP :, :].astype(F32).reshape(blocks * GROUP, rows)
    for c0 in range(0, GROUP, STEP):
        h = spectrum(wide, 0, c0, enter_ref, fwd_h, fwd_l, cos_t, sin_t)
        h_ref[c0 * blocks : (c0 + STEP) * blocks, :] = h
        out = signal(*plain_product(h, chunk(v_ref, c0, blocks)), leave_ref, inv_h, inv_l, cos_t, sin_t)
        for c in range(STEP):
            result[pl.ds(c0 + c, blocks, stride=GROUP), :] = out[:, c * rows : (c + 1) * rows]
    out_ref[...] = result[...].astype(BF16).reshape(blocks, GROUP, rows)


def back_kernel(
    conv_ref, h_ref, g_ref, leave_ref, inv_h, inv_l, cos_ref, sin_ref, *rest
):
    pieces, (out_ref, result, tail) = rest[:SHARES], rest[SHARES:]
    blocks, rows = conv_ref.shape[0], conv_ref.shape[2]
    cos_t, sin_t = cos_ref[...], sin_ref[...]
    for c0 in range(0, GROUP, STEP):
        out = signal(
            *conj_product(chunk(h_ref, c0, blocks), chunk(g_ref, c0, blocks)),
            leave_ref, inv_h, inv_l, cos_t, sin_t,
        )
        for c in range(STEP):
            result[pl.ds(c0 + c, blocks, stride=GROUP), :] = out[:, c * rows : (c + 1) * rows]
    out_ref[:, :GROUP, :] = conv_ref[...]
    out_ref[:, GROUP : 2 * GROUP, :] = result[...].astype(BF16).reshape(blocks, GROUP, rows)
    tail[...] = jnp.zeros_like(tail)
    for c in range(STEP):
        total = pieces[0][c].astype(F32)
        for piece in pieces[1:]:
            total = total + piece[c].astype(F32)
        tail[pl.ds(c, blocks, stride=TAIL), :] = total
    out_ref[:, 2 * GROUP :, :] = tail[...].astype(BF16).reshape(blocks, TAIL, rows)


def finish_kernel(values_ref, gates_ref, grad_ref, skip_ref, in_ref, value_out, gate_out, filter_out, flat, mixed):
    blocks, rows = in_ref.shape[0], in_ref.shape[2]
    share = GROUP // SHARES

    def part(a):
        mixed[a] = in_ref[:, a * GROUP : (a + 1) * GROUP, :].astype(F32).reshape(-1, rows)
        for q in range(SHARES):
            for i in range(share):
                row = mixed[a, pl.ds(q * share + i, blocks, stride=GROUP), :]
                flat[a, pl.ds(q * share * blocks + i, blocks, stride=share), :] = row
        return flat[a].T

    grad = grad_ref[...]
    skip = skip_ref[...]
    gate_out[...] = (grad * (part(0) + skip * values_ref[...].astype(F32))).astype(BF16)
    gate_term = (grad * gates_ref[...].astype(F32)).astype(BF16).astype(F32)
    value_out[...] = (part(1) + skip * gate_term).astype(BF16)
    tail = in_ref[:, 2 * GROUP :, :].astype(F32).reshape(-1, rows)
    mixed[0, : blocks * TAIL, :] = tail
    for i in range(share):
        row = mixed[0, pl.ds(i, blocks, stride=TAIL), :]
        flat[0, pl.ds(i, blocks, stride=share), :] = row
    filter_out[...] = flat[0, : blocks * share, :].T


def call(kernel, out_shape, args, scratch, specs=None):
    outs = jax.tree.map(lambda _: VMEM, out_shape)
    return pl.pallas_call(
        kernel,
        out_shape=out_shape,
        in_specs=specs or [VMEM] * len(args),
        out_specs=outs,
        scratch_shapes=scratch,
        compiler_params=pltpu.CompilerParams(vmem_limit_bytes=48 * 1024 * 1024),
    )(*args)


def transforms(held, rank, consts, exchange):
    blocks, _, rows = held.shape
    enter, leave, fwd_h, fwd_l, inv_h, inv_l, cos_t, sin_t = consts
    piece = jax.ShapeDtypeStruct((STEP, blocks, rows), BF16)
    spec = jax.ShapeDtypeStruct((GROUP * blocks, 2 * rows), F32)
    wide = pltpu.VMEM((GROUP * blocks, rows), F32)
    *pieces, v, g = call(
        terms_kernel,
        (piece,) * SHARES + (spec, spec),
        (rank, held, *consts),
        [pltpu.VMEM((2, GROUP * blocks, rows), F32)],
        [pl.BlockSpec(memory_space=pltpu.SMEM)] + [VMEM] * 9,
    )
    pieces = exchange(pieces)
    conv, h = call(
        conv_kernel,
        (jax.ShapeDtypeStruct((blocks, GROUP, rows), BF16), spec),
        (held, v, *consts),
        [pltpu.VMEM((1, GROUP * blocks, rows), F32), wide],
    )
    return call(
        back_kernel,
        jax.ShapeDtypeStruct((blocks, 2 * GROUP + TAIL, rows), BF16),
        (conv, h, g, leave, inv_h, inv_l, cos_t, sin_t, *pieces),
        [wide, pltpu.VMEM((TAIL * blocks, rows), F32)],
    )


def local(values, gates, grad_out, filter_raw, skip_gain):
    rows, width = values.shape
    blocks = lax.axis_size("seq")
    rank = lax.axis_index("chan").astype(jnp.int32).reshape(1)
    flat = pltpu.VMEM((3, width, rows), F32)
    sent = call(
        pack_kernel,
        jax.ShapeDtypeStruct((blocks, 3 * GROUP, rows), BF16),
        (values, gates, grad_out, filter_raw),
        [
            pltpu.VMEM((rows, width), BF16),
            pltpu.VMEM((rows, width), BF16),
            pltpu.VMEM((rows, width), F32),
            pltpu.VMEM((rows, width), BF16),
            flat,
            flat,
            pltpu.SemaphoreType.DMA((4,)),
        ],
        [pl.BlockSpec(memory_space=pl.ANY)] * 4,
    )
    held = lax.all_to_all(sent, "seq", split_axis=0, concat_axis=0, tiled=True)

    def exchange(pieces):
        return [pieces[0]] + [
            lax.ppermute(pieces[d], "chan", [(src, (src + d) % SHARES) for src in range(SHARES)])
            for d in range(1, SHARES)
        ]

    done = transforms(held, rank, tables(blocks, rows), exchange)
    back = lax.all_to_all(done, "seq", split_axis=0, concat_axis=0, tiled=True)
    shape = jax.ShapeDtypeStruct((rows, width), BF16)
    pair = pltpu.VMEM((2, width, rows), F32)
    return call(
        finish_kernel,
        (shape, shape, jax.ShapeDtypeStruct((rows, width // SHARES), F32)),
        (values, gates, grad_out, skip_gain[None, :], back),
        [pair, pair],
    )


def solution(mesh):
    in_specs = (P("seq", "chan"), P("seq", "chan"), P("seq", "chan"), P("seq", None), P("chan"))
    out_specs = (P("seq", "chan"), P("seq", "chan"), P("seq", "chan"))
    return jax.shard_map(local, mesh=mesh, in_specs=in_specs, out_specs=out_specs, check_vma=False)
```

time: 95.7 us -> 92.2 us (0.963)
  blocking collectives: 37.6 us -> 27.9 us
  starting transfers between devices: 16.9 us -> 24.8 us
  waiting for transfers between devices: 24.3 us -> 22.1 us
    all_to_all x1, blocking collectives: 37.6 us -> 27.9 us  [local(): back = lax.all_to_all(done, 'seq', split_axis=0, concat_axis=0, tiled=True)]
    all_to_all x1, starting transfers between devices: 7.54 us -> 15.8 us  [local(): held = lax.all_to_all(sent, 'seq', split_axis=0, concat_axis=0, tiled=True)]
    ppermute x3, waiting for transfers between devices: 1.36 us -> 0.01 us  [exchange(): lax.ppermute(pieces[d], 'chan', [(src, (src + d) % SHARES) for src in ran...]
    pallas_call x4 -> x5, Pallas kernels: 11.5 us -> 12.1 us  [call(): pl.pallas_call(kernel, out_shape=out_shape, in_specs=specs or [VMEM] * le...]
  transfers between devices with their start and end apart: 4 -> 4, of which waited for: 2 -> 1; matrix products, arithmetic and copies ran while one was open for 0% -> 0% of each run, Pallas kernels for 1% -> 4%
where the time goes in v2:
time: 92.2 us; the launch traced here: 91.7 us
  blocking collectives  27.9 us (30%)
  starting transfers between devices  24.8 us (27%)
  waiting for transfers between devices  22.1 us (24%)
  Pallas kernels  12.1 us (13%)
  local copies, waits for them, and re-layouts  3.97 us (4%)
    all_to_all x1, blocking collectives, local(): back = lax.all_to_all(done, 'seq', split_axis=0, concat_axis=0, tiled=True)  27.9 us
    all_to_all x1, waiting for transfers between devices, local(): held = lax.all_to_all(sent, 'seq', split_axis=0, concat_axis=0, tiled=True)  22 us
    all_to_all x1, starting transfers between devices, local(): held = lax.all_to_all(sent, 'seq', split_axis=0, concat_axis=0, tiled=True)  15.8 us
    pallas_call x5, Pallas kernels, call(): pl.pallas_call(kernel, out_shape=out_shape, in_specs=specs or [VMEM] * le...  12.1 us
    ppermute x3, starting transfers between devices, exchange(): lax.ppermute(pieces[d], 'chan', [(src, (src + d) % SHARES) for src in ran...  9.05 us
    unnamed x32, local copies, waits for them, and re-layouts  3.97 us
  transfers between devices with their start and end apart: 4, of which 1 were waited for; matrix products, arithmetic and copies ran while one was open for 0% of the time, Pallas kernels for 4%

profile of v2, /device:TPU:1, one launch (start us, length us, event | category | flops | bytes accessed | tf_op | source)
XLA Modules:
  0.0 91.7 jit_solution(13475775855984622561)
XLA Ops:
  0.6 0.0 copy-start
  0.6 1.0 %copy-done = f32[128,1024]{1,0:T(8,128)S(1)} copy-done((f32[128,1024]{1,0:T(8,128)S(1)}, f32[128,1024]{1,0:T(8,128)}, u32[]{:S(2)}) %copy-start) | copy-done | bytes 524312
  1.7 0.0 copy-start.4
  1.7 0.9 %copy-done.4 = bf16[128,1024]{1,0:T(8,128)(2,1)S(1)} copy-done((bf16[128,1024]{1,0:T(8,128)(2,1)S(1)}, bf16[128,1024]{1,0:T(8,128)(2,1)}, u32[]{:S(2)}) %copy-start.4) | copy-done | bytes 262168
  2.6 0.0 copy-start.6
  2.6 0.9 %copy-done.6 = bf16[128,1024]{1,0:T(8,128)(2,1)S(1)} copy-done((bf16[128,1024]{1,0:T(8,128)(2,1)S(1)}, bf16[128,1024]{1,0:T(8,128)(2,1)}, u32[]{:S(2)}) %copy-start.6) | copy-done | bytes 262168
  3.6 0.0 copy-start.13
  3.6 0.9 %copy-done.13 = bf16[128,1024]{1,0:T(8,128)(2,1)S(1)} copy-done((bf16[128,1024]{1,0:T(8,128)(2,1)S(1)}, bf16[128,1024]{1,0:T(8,128)(2,1)}, u32[]{:S(2)}) %copy-start.13) | copy-done | bytes 262168
  4.5 2.0 %shard_map.148 = bf16[64,48,128]{2,1,0:T(8,128)(2,1)} custom-call(bf16[128,1024]{1,0:T(8,128)(2,1)S(1)} %copy-done.4, bf16[128,1024]{1,0:T(8,128)(2,1)S(1)} %copy-done.6, f32[128,1024]{1,0:T(8,128)S(1)} %copy-done, bf16[128,1024]{1,0:T(8,128)(2,1)S(1)} %copy-done.13), custom_call_target="tpu_custom_call" | custom-call | tf_op jit(solution)/shard_map/pallas_call | solution.py:237
  6.5 0.0 copy-start.2
  6.5 0.0 copy-start.3
  6.6 0.0 copy-start.8
  6.6 0.0 copy-start.9
  6.6 0.0 copy-start.10
  6.6 0.0 copy-start.11
  6.6 0.0 copy-start.12
  6.6 0.0 copy-start.14
  6.6 15.8 %all-to-all-start = ((bf16[64,48,128]{2,1,0:T(8,128)(2,1)}), bf16[64,48,128]{2,1,0:T(8,128)(2,1)S(1)}, u32[]{:S(2)}, u32[]{:S(2)}) async-start(bf16[64,48,128]{2,1,0:T(8,128)(2,1)} %shard_map.148), calls=%async_computation | async-start | bytes 1572864 | tf_op jit(solution)/shard_map/all_to_all | solution.py:295
  22.4 22.0 %all-to-all-done.in_ref = bf16[64,48,128]{2,1,0:T(8,128)(2,1)S(1)} async-done(((bf16[64,48,128]{2,1,0:T(8,128)(2,1)}), bf16[64,48,128]{2,1,0:T(8,128)(2,1)S(1)}, u32[]{:S(2)}, u32[]{:S(2)}) %all-to-all-start) | async-done | bytes 786464 | tf_op jit(solution)/shard_map/all_to_all | solution.py:295
  44.4 0.0 copy-done.2
  44.5 0.0 copy-done.3
  44.5 0.0 copy-done.8
  44.5 0.0 copy-done.9
  44.5 0.0 copy-done.10
  44.5 0.0 copy-done.11
  44.5 0.0 copy-done.12
  44.5 0.0 copy-done.14
  44.5 3.6 %shard_map.149 = (bf16[4,64,128]{2,1,0:T(8,128)(2,1)S(1)}, bf16[4,64,128]{2,1,0:T(8,128)(2,1)S(1)}, bf16[4,64,128]{2,1,0:T(8,128)(2,1)S(1)}, bf16[4,64,128]{2,1,...) custom-call(s32[1]{0:T(128)} %bitcast.1.rank_ref, bf16[64,48,128]{2,1,0:T(8,128)(2,1)S(1)} %all-to-all-done.in_ref, ...), custom_call_target="tpu_custom_call" | custom-call | tf_op jit(solution)/shard_map/pallas_call | solution.py:237
  48.1 6.2 %collective-permute-start = (bf16[4,64,128]{2,1,0:T(8,128)(2,1)S(1)}, bf16[4,64,128]{2,1,0:T(8,128)(2,1)S(1)}, u32[]{:S(2)}, u32[]{:S(2)}) collective-permute-start(bf16[4,64,128]{2,1,0:T(8,128)(2,1)S(1)} %get-tuple-element.16), channel_id=1, source_target_pairs={{0,1},{1,2},{2,3},{3,0},{4,5},{5,6},{6,7},{7,4},{8,9},{9,10},{10,1... | collective-permute-start | bytes 196616 | tf_op jit(solution)/shard_map/ppermute | solution.py:299
  54.3 0.6 collective-permute-start.1
  54.9 2.3 %collective-permute-start.2 = (bf16[4,64,128]{2,1,0:T(8,128)(2,1)S(1)}, bf16[4,64,128]{2,1,0:T(8,128)(2,1)S(1)}, u32[]{:S(2)}, u32[]{:S(2)}) collective-permute-start(bf16[4,64,128]{2,1,0:T(8,128)(2,1)S(1)} %get-tuple-element.18), channel_id=1, source_target_pairs={{0,3},{1,0},{2,1},{3,2},{4,7},{5,4},{6,5},{7,6},{8,11},{9,8},{10,9... | collective-permute-start | bytes 196616 | tf_op jit(solution)/shard_map/ppermute | solution.py:299
  57.2 3.4 %shard_map.150 = (bf16[64,16,128]{2,1,0:T(8,128)(2,1)S(1)}, f32[1024,256]{1,0:T(8,128)S(1)}) custom-call(bf16[64,48,128]{2,1,0:T(8,128)(2,1)S(1)} %all-to-all-done.in_ref, f32[1024,256]{1,0:T(8,128)S(1)} %get-tuple-element.11.v_ref, bf16[256,64]{1,0:T(8,128)(2,1)S(1)} %copy-done.14, bf16[128,128]{1,0:T(8,128)(2,1)S(1)} %copy-done.12, ...), custom_call_target="tpu_custom_call" | custom-call | tf_op jit(solution)/shard_map/pallas_call | solution.py:237
  60.6 0.0 collective-permute-done.rest_1_
  60.6 0.0 collective-permute-done.1.rest_2_
  60.6 0.0 collective-permute-done.2.rest_3_
  60.6 1.7 %shard_map.151 = bf16[64,40,128]{2,1,0:T(8,128)(2,1)S(1)} custom-call(bf16[64,16,128]{2,1,0:T(8,128)(2,1)S(1)} %get-tuple-element.12.conv_ref, f32[1024,256]{1,0:T(8,128)S(1)} %get-tuple-element.13.h_ref, f32[1024,256]{1,0:T(8,128)S(1)} %get-tuple-element.14.g_ref, bf16[128,128]{1,0:T(8,128)(2,1)S(1)} %copy-done.12, bf16[256,256]{1,0:T(8,128)(2,1)S(1)} %copy-done.3, ...), custom_call_target="tpu_custom_call" | custom-call | tf_op jit(solution)/shard_map/pallas_call | solution.py:237
  62.3 0.0 copy-start.1
  62.3 0.0 copy-start.5
  62.3 0.0 copy-start.7
  62.3 0.0 copy-start.15
  62.3 27.9 %all_to_all.10.in_ref = bf16[64,40,128]{2,1,0:T(8,128)(2,1)S(1)} all-to-all(bf16[64,40,128]{2,1,0:T(8,128)(2,1)S(1)} %shard_map.151), channel_id=1, replica_groups=mesh['seq'=64,'chan'=4] {'seq'}, dimensions={0} | all-to-all | bytes 1310720 | tf_op jit(solution)/shard_map/all_to_all | solution.py:304
  90.2 0.0 copy-done.1
  90.2 0.0 copy-done.5
  90.2 0.0 copy-done.7
  90.2 0.0 copy-done.15
  90.3 1.5 %shard_map.152 = (bf16[128,1024]{1,0:T(8,128)(2,1)}, bf16[128,1024]{1,0:T(8,128)(2,1)}, f32[128,256]{1,0:T(8,128)}) custom-call(bf16[128,1024]{1,0:T(8,128)(2,1)S(1)} %copy-done.5, bf16[128,1024]{1,0:T(8,128)(2,1)S(1)} %copy-done.7, f32[128,1024]{1,0:T(8,128)S(1)} %copy-done.1, f32[1,1024]{1,0:T(1,128)S(1)} %bitcast.2, ...), custom_call_target="tpu_custom_call" | custom-call | tf_op jit(solution)/shard_map/pallas_call | solution.py:237
Async XLA Ops:
  0.6 1.0 %copy-start = (f32[128,1024]{1,0:T(8,128)S(1)}, f32[128,1024]{1,0:T(8,128)}, u32[]{:S(2)}) copy-start(f32[128,1024]{1,0:T(8,128)} %grad_ref.3) | copy-start | bytes 1572868
  1.7 0.9 %copy-start.4 = (bf16[128,1024]{1,0:T(8,128)(2,1)S(1)}, bf16[128,1024]{1,0:T(8,128)(2,1)}, u32[]{:S(2)}) copy-start(bf16[128,1024]{1,0:T(8,128)(2,1)} %values_ref.3) | copy-start | bytes 786436
  2.6 0.9 %copy-start.6 = (bf16[128,1024]{1,0:T(8,128)(2,1)S(1)}, bf16[128,1024]{1,0:T(8,128)(2,1)}, u32[]{:S(2)}) copy-start(bf16[128,1024]{1,0:T(8,128)(2,1)} %gates_ref.3) | copy-start | bytes 786436
  3.6 0.9 %copy-start.13 = (bf16[128,1024]{1,0:T(8,128)(2,1)S(1)}, bf16[128,1024]{1,0:T(8,128)(2,1)}, u32[]{:S(2)}) copy-start(bf16[128,1024]{1,0:T(8,128)(2,1)} %filter_ref.1) | copy-start | bytes 786436
  6.5 37.9 %copy-start.2 = (bf16[256,256]{1,0:T(8,128)(2,1)S(1)}, bf16[256,256]{1,0:T(8,128)(2,1)}, u32[]{:S(2)}) copy-start(bf16[256,256]{1,0:T(8,128)(2,1)} %constant.25.clone.inv_l) | copy-start | bytes 393220
  6.5 37.9 %copy-start.3 = (bf16[256,256]{1,0:T(8,128)(2,1)S(1)}, bf16[256,256]{1,0:T(8,128)(2,1)}, u32[]{:S(2)}) copy-start(bf16[256,256]{1,0:T(8,128)(2,1)} %constant.24.clone.inv_h) | copy-start | bytes 393220
  6.6 37.9 %copy-start.8 = (bf16[256,256]{1,0:T(8,128)(2,1)S(1)}, bf16[256,256]{1,0:T(8,128)(2,1)}, u32[]{:S(2)}) copy-start(bf16[256,256]{1,0:T(8,128)(2,1)} %constant.23.clone.fwd_l) | copy-start | bytes 393220
  6.6 37.9 %copy-start.9 = (bf16[256,256]{1,0:T(8,128)(2,1)S(1)}, bf16[256,256]{1,0:T(8,128)(2,1)}, u32[]{:S(2)}) copy-start(bf16[256,256]{1,0:T(8,128)(2,1)} %constant.22.clone.fwd_h) | copy-start | bytes 393220
  6.6 37.9 %copy-start.10 = (f32[64,128]{1,0:T(8,128)S(1)}, f32[64,128]{1,0:T(8,128)}, u32[]{:S(2)}) copy-start(f32[64,128]{1,0:T(8,128)} %constant.27.clone.sin_ref) | copy-start | bytes 98308
  6.6 37.9 %copy-start.11 = (f32[64,128]{1,0:T(8,128)S(1)}, f32[64,128]{1,0:T(8,128)}, u32[]{:S(2)}) copy-start(f32[64,128]{1,0:T(8,128)} %constant.26.clone.cos_ref) | copy-start | bytes 98308
  6.6 37.9 %copy-start.12 = (bf16[128,128]{1,0:T(8,128)(2,1)S(1)}, bf16[128,128]{1,0:T(8,128)(2,1)}, u32[]{:S(2)}) copy-start(bf16[128,128]{1,0:T(8,128)(2,1)} %constant.21.clone.leave_ref) | copy-start | bytes 98308
  6.6 37.9 %copy-start.14 = (bf16[256,64]{1,0:T(8,128)(2,1)S(1)}, bf16[256,64]{1,0:T(8,128)(2,1)}, u32[]{:S(2)}) copy-start(bf16[256,64]{1,0:T(8,128)(2,1)} %constant.20.clone.enter_ref) | copy-start | bytes 98308
  6.6 37.8 %all-to-all-start = ((bf16[64,48,128]{2,1,0:T(8,128)(2,1)}), bf16[64,48,128]{2,1,0:T(8,128)(2,1)S(1)}, u32[]{:S(2)}, u32[]{:S(2)}) async-start(bf16[64,48,128]{2,1,0:T(8,128)(2,1)} %shard_map.148), calls=%async_computation | async-start | bytes 1572864 | tf_op jit(solution)/shard_map/all_to_all | solution.py:295
  48.1 12.5 %collective-permute-start = (bf16[4,64,128]{2,1,0:T(8,128)(2,1)S(1)}, bf16[4,64,128]{2,1,0:T(8,128)(2,1)S(1)}, u32[]{:S(2)}, u32[]{:S(2)}) collective-permute-start(bf16[4,64,128]{2,1,0:T(8,128)(2,1)S(1)} %get-tuple-element.16), channel_id=1, source_target_pairs={{0,1},{1,2},{2,3},{3,0},{4,5},{5,6},{6,7},{7,4},{8,9},{9,10},{10,1... | collective-permute-start | bytes 196616 | tf_op jit(solution)/shard_map/ppermute | solution.py:299
  54.3 6.2 %collective-permute-start.1 = (bf16[4,64,128]{2,1,0:T(8,128)(2,1)S(1)}, bf16[4,64,128]{2,1,0:T(8,128)(2,1)S(1)}, u32[]{:S(2)}, u32[]{:S(2)}) collective-permute-start(bf16[4,64,128]{2,1,0:T(8,128)(2,1)S(1)} %get-tuple-element.17), channel_id=1, source_target_pairs={{0,2},{1,3},{2,0},{3,1},{4,6},{5,7},{6,4},{7,5},{8,10},{9,11},{10,... | collective-permute-start | bytes 196616 | tf_op jit(solution)/shard_map/ppermute | solution.py:299
  54.9 5.7 %collective-permute-start.2 = (bf16[4,64,128]{2,1,0:T(8,128)(2,1)S(1)}, bf16[4,64,128]{2,1,0:T(8,128)(2,1)S(1)}, u32[]{:S(2)}, u32[]{:S(2)}) collective-permute-start(bf16[4,64,128]{2,1,0:T(8,128)(2,1)S(1)} %get-tuple-element.18), channel_id=1, source_target_pairs={{0,3},{1,0},{2,1},{3,2},{4,7},{5,4},{6,5},{7,6},{8,11},{9,8},{10,9... | collective-permute-start | bytes 196616 | tf_op jit(solution)/shard_map/ppermute | solution.py:299
  62.3 28.0 %copy-start.1 = (f32[128,1024]{1,0:T(8,128)S(1)}, f32[128,1024]{1,0:T(8,128)}, u32[]{:S(2)}) copy-start(f32[128,1024]{1,0:T(8,128)} %grad_ref.3) | copy-start | bytes 1572868
  62.3 27.9 %copy-start.5 = (bf16[128,1024]{1,0:T(8,128)(2,1)S(1)}, bf16[128,1024]{1,0:T(8,128)(2,1)}, u32[]{:S(2)}) copy-start(bf16[128,1024]{1,0:T(8,128)(2,1)} %values_ref.3) | copy-start | bytes 786436
  62.3 27.9 %copy-start.7 = (bf16[128,1024]{1,0:T(8,128)(2,1)S(1)}, bf16[128,1024]{1,0:T(8,128)(2,1)}, u32[]{:S(2)}) copy-start(bf16[128,1024]{1,0:T(8,128)(2,1)} %gates_ref.3) | copy-start | bytes 786436
  62.3 27.9 %copy-start.15 = (f32[1024]{0:T(1024)S(1)}, f32[1024]{0:T(1024)}, u32[]{:S(2)}) copy-start(f32[1024]{0:T(1024)} %param.17) | copy-start | bytes 12292

commit v3 on v1

v3 whole, which is shorter than its diff:
```python
import math

import jax
import jax.numpy as jnp
import numpy as np
from jax import lax
from jax.experimental import pallas as pl
from jax.experimental.pallas import tpu as pltpu
from jax.sharding import PartitionSpec as P

F32 = jnp.float32
BF16 = jnp.bfloat16
VMEM = pl.BlockSpec(memory_space=pltpu.VMEM)
SHARE = 4
SENT = 10
BACK = 12
WIDE = True


def split_pair(table):
    high = table.astype(np.float32).astype(jnp.bfloat16)
    low = (table - high.astype(np.float64)).astype(np.float32).astype(jnp.bfloat16)
    return high, low


def tables(blocks, rows):
    period = 2 * blocks * rows
    scale = 2.0 / period / math.sqrt(blocks * rows)
    half = np.arange(blocks) + 0.5
    block_angle = 2.0 * np.pi / (2 * blocks) * np.outer(half, np.arange(blocks))
    enter = np.concatenate([np.cos(block_angle), -np.sin(block_angle)], axis=0)
    leave = np.concatenate([np.cos(block_angle), -np.sin(block_angle)], axis=0).T * scale
    turn = 2.0 * np.pi / period * np.outer(half, np.arange(rows))
    row_angle = 2.0 * np.pi / rows * np.outer(np.arange(rows), np.arange(rows))
    row_cos, row_sin = np.cos(row_angle), np.sin(row_angle)
    forward = np.block([[row_cos, -row_sin], [row_sin, row_cos]])
    inverse = np.block([[row_cos, row_sin], [-row_sin, row_cos]])
    enter_pair = np.concatenate(split_pair(enter), axis=0)
    leave_high, leave_low = split_pair(leave)
    leave_pair = np.concatenate([leave_high, leave_low], axis=0)
    if not WIDE:
        enter_pair, leave_pair = enter_pair[: 2 * blocks], leave_pair[:blocks]
    return (
        enter_pair,
        leave_pair,
        *split_pair(forward),
        *split_pair(inverse),
        np.cos(turn).astype(np.float32),
        np.sin(turn).astype(np.float32),
    )


def split_value(x):
    high = x.astype(BF16)
    return high, (x - high.astype(F32)).astype(BF16)


def dot(a, b):
    return jnp.dot(a, b, preferred_element_type=F32)


def dot_wide(x, high, low):
    if not WIDE:
        return dot(x.astype(BF16), high)
    x_high, x_low = split_value(x)
    return dot(x_high, high) + (dot(x_low, high) + dot(x_high, low))


def pack_kernel(rank_ref, values_ref, gates_ref, grad_ref, filter_ref, out_ref, values, gates, grad, taps, flat, rows_ref, sems):
    pairs = flat.shape[0] // SHARE
    copies = [
        pltpu.make_async_copy(src, dst, sems.at[k])
        for k, (src, dst) in enumerate(
            ((values_ref, values), (filter_ref, taps), (gates_ref, gates), (grad_ref, grad))
        )
    ]
    for copy in copies:
        copy.start()

    def place(part, sources, start):
        flat[...] = part.T
        for k, source in enumerate(sources):
            rows_ref[pl.ds(start + k, pairs, stride=SENT), :] = flat[
                pl.ds(source, pairs, stride=SHARE), :
            ]

    copies[0].wait()
    place(values[...].astype(F32), range(SHARE), 0)
    copies[1].wait()
    place(taps[...].astype(F32), (rank_ref[0], rank_ref[0]), 2 * SHARE)
    copies[2].wait()
    copies[3].wait()
    gate_term = (grad[...] * gates[...].astype(F32)).astype(BF16).astype(F32)
    place(gate_term, range(SHARE), SHARE)
    out_ref[...] = rows_ref[...].astype(BF16)


def spectra_kernel(
    in_ref, enter_ref, leave_ref, fwd_h, fwd_l, inv_h, inv_l, cos_ref, sin_ref, out_ref, wide, result
):
    blocks, rows = cos_ref.shape
    copies = in_ref.shape[0] // (blocks * SENT)
    cos_t, sin_t = cos_ref[...], sin_ref[...]
    wide[...] = in_ref[...].astype(F32)

    def spectrum(starts):
        cols = [wide[pl.ds(start, blocks, stride=SENT), :] for start in starts]
        mixed = dot(enter_ref[...], jnp.concatenate(cols, axis=1).astype(BF16))
        if WIDE:
            mixed = mixed[: 2 * blocks] + mixed[2 * blocks :]
        turned = []
        for c in range(SHARE):
            re = mixed[:blocks, c * rows : (c + 1) * rows]
            im = mixed[blocks:, c * rows : (c + 1) * rows]
            turned.append(
                jnp.concatenate([re * cos_t + im * sin_t, im * cos_t - re * sin_t], axis=1)
            )
        full = dot_wide(jnp.concatenate(turned, axis=0), fwd_h[...], fwd_l[...])
        return full[:, :rows], full[:, rows:]

    def signal(re, im):
        full = dot_wide(jnp.concatenate([re, im], axis=1), inv_h[...], inv_l[...])
        cols = []
        for c in range(SHARE):
            re = full[c * blocks : (c + 1) * blocks, :rows]
            im = full[c * blocks : (c + 1) * blocks, rows:]
            cols.append(
                jnp.concatenate([re * cos_t - im * sin_t, re * sin_t + im * cos_t], axis=0)
            )
        joined = jnp.concatenate(cols, axis=1)
        if not WIDE:
            mixed = dot(leave_ref[...], joined.astype(BF16))
        else:
            high, low = split_value(joined)
            pair = dot(leave_ref[...], high)
            mixed = pair[:blocks] + (pair[blocks:] + dot(leave_ref[:blocks, :], low))
        return [mixed[:, c * rows : (c + 1) * rows] for c in range(SHARE)]

    def put(block, first, cols):
        for c, col in enumerate(cols):
            result[pl.ds(block * blocks * BACK + first + c, blocks, stride=BACK), :] = col

    h_re, h_im = spectrum([c * blocks * SENT + 2 * SHARE for c in range(SHARE)])
    f_re = f_im = None
    for j in range(copies):
        base = j * blocks * SENT
        v_re, v_im = spectrum([base + c for c in range(SHARE)])
        put(j, 0, signal(h_re * v_re - h_im * v_im, h_re * v_im + h_im * v_re))
        g_re, g_im = spectrum([base + SHARE + c for c in range(SHARE)])
        put(j, SHARE, signal(h_re * g_re + h_im * g_im, h_re * g_im - h_im * g_re))
        re, im = v_re * g_re + v_im * g_im, v_re * g_im - v_im * g_re
        f_re, f_im = (re, im) if j == 0 else (f_re + re, f_im + im)
    terms = signal(f_re, f_im)
    for j in range(copies):
        put(j, 2 * SHARE, terms)
    out_ref[...] = result[...].astype(BF16)


def finish_kernel(
    rank_ref, values_ref, gates_ref, grad_ref, skip_ref, in_ref, value_out, gate_out, filter_out, wide, flat
):
    pairs = flat.shape[0] // SHARE
    own = filter_out.shape[1]
    wide[...] = in_ref[...].astype(F32)

    def part(first):
        for c in range(SHARE):
            flat[pl.ds(c, pairs, stride=SHARE), :] = wide[pl.ds(first + c, pairs, stride=BACK), :]
        return flat[...].T

    grad = grad_ref[...]
    skip = skip_ref[...]
    gate_out[...] = (grad * (part(0) + skip * values_ref[...].astype(F32))).astype(BF16)
    gate_term = (grad * gates_ref[...].astype(F32)).astype(BF16).astype(F32)
    value_out[...] = (part(SHARE) + skip * gate_term).astype(BF16)
    start = rank_ref[0] * (own // SHARE * BACK) + 2 * SHARE
    for c in range(SHARE):
        flat[pl.ds(c, own // SHARE, stride=SHARE), :] = wide[
            pl.ds(start + c, own // SHARE, stride=BACK), :
        ]
    filter_out[...] = flat[:own, :].T


def call(kernel, out_shape, args, scratch, specs=None, limit=48):
    return pl.pallas_call(
        kernel,
        out_shape=out_shape,
        in_specs=specs or [VMEM] * len(args),
        out_specs=jax.tree.map(lambda _: VMEM, out_shape),
        scratch_shapes=scratch,
        compiler_params=pltpu.CompilerParams(vmem_limit_bytes=limit * 1024 * 1024),
    )(*args)


def exchange(x):
    shaped = x.reshape(lax.axis_size("chan") * lax.axis_size("seq"), -1, 2, x.shape[1])
    moved = lax.all_to_all(shaped, ("chan", "seq"), split_axis=0, concat_axis=0, tiled=True)
    return moved.reshape(x.shape)


def transform(held, blocks):
    rows = held.shape[1]
    back = held.shape[0] // SENT * BACK
    consts = tables(blocks, rows)
    return call(
        spectra_kernel,
        jax.ShapeDtypeStruct((back, rows), BF16),
        (held, *consts),
        [pltpu.VMEM(held.shape, F32), pltpu.VMEM((back, rows), F32)],
    )


def local(values, gates, grad_out, filter_raw, skip_gain):
    rows, width = values.shape
    blocks = lax.axis_size("seq")
    pairs = blocks * lax.axis_size("chan")
    rank = lax.axis_index("chan").astype(jnp.int32).reshape(1)
    flat = pltpu.VMEM((width, rows), F32)
    scalar = pl.BlockSpec(memory_space=pltpu.SMEM)
    sent = call(
        pack_kernel,
        jax.ShapeDtypeStruct((pairs * SENT, rows), BF16),
        (rank, values, gates, grad_out, filter_raw),
        [
            pltpu.VMEM((rows, width), BF16),
            pltpu.VMEM((rows, width), BF16),
            pltpu.VMEM((rows, width), F32),
            pltpu.VMEM((rows, width), BF16),
            flat,
            pltpu.VMEM((pairs * SENT, rows), F32),
            pltpu.SemaphoreType.DMA((4,)),
        ],
        [scalar] + [pl.BlockSpec(memory_space=pltpu.HBM)] * 4,
        limit=60,
    )
    back = exchange(transform(exchange(sent), blocks))
    shape = jax.ShapeDtypeStruct((rows, width), BF16)
    return call(
        finish_kernel,
        (shape, shape, jax.ShapeDtypeStruct((rows, width // lax.axis_size("chan")), F32)),
        (rank, values, gates, grad_out, skip_gain[None, :], back),
        [pltpu.VMEM(back.shape, F32), flat],
        [scalar] + [VMEM] * 5,
    )


def solution(mesh):
    in_specs = (P("seq", "chan"), P("seq", "chan"), P("seq", "chan"), P("seq", None), P("chan"))
    out_specs = (P("seq", "chan"), P("seq", "chan"), P("seq", "chan"))
    return jax.shard_map(local, mesh=mesh, in_specs=in_specs, out_specs=out_specs, check_vma=False)
```

time: 95.7 us -> 82.2 us (0.86)
  blocking collectives: 37.6 us -> 70.4 us
  waiting for transfers between devices: 24.3 us -> 0 us
  starting transfers between devices: 16.9 us -> 0 us
  local copies, waits for them, and re-layouts: 4.01 us -> 0.08 us
    all_to_all x1 -> x2, blocking collectives: 37.6 us -> 70.4 us  [exchange(): lax.all_to_all(shaped, ('chan', 'seq'), split_axis=0, concat_axis=0, tile...]
    all_to_all x1 -> x0, waiting for transfers between devices: 22.9 us -> none  [local(): back = lax.all_to_all(done, 'seq', split_axis=0, concat_axis=0, tiled=True)]
    ppermute x3 -> x0, starting transfers between devices: 9.34 us -> none  [local(): lax.ppermute(pieces[d], 'chan', [(src, (src + d) % copies) for src in ran...]
    all_to_all x1 -> x0, starting transfers between devices: 7.54 us -> none  [local(): back = lax.all_to_all(done, 'seq', split_axis=0, concat_axis=0, tiled=True)]
    unnamed x32 -> x24, local copies, waits for them, and re-layouts: 3.97 us -> 0.08 us
    ppermute x3 -> x0, waiting for transfers between devices: 1.36 us -> none  [local(): lax.ppermute(pieces[d], 'chan', [(src, (src + d) % copies) for src in ran...]
    pallas_call x4 -> x3, Pallas kernels: 11.5 us -> 10.7 us  [call(): pl.pallas_call(kernel, out_shape=out_shape, in_specs=specs or [VMEM] * le...]
  transfers between devices with their start and end apart: 4 -> 0, of which waited for: 2 -> 0; matrix products, arithmetic and copies ran while one was open for 0% -> 0% of each run, Pallas kernels for 1% -> 0%
where the time goes in v3:
time: 82.2 us; the launch traced here: 82 us
  blocking collectives  70.4 us (86%)
  Pallas kernels  10.7 us (13%)
    all_to_all x2, blocking collectives, exchange(): lax.all_to_all(shaped, ('chan', 'seq'), split_axis=0, concat_axis=0, tile...  70.4 us
    pallas_call x3, Pallas kernels, call(): pl.pallas_call(kernel, out_shape=out_shape, in_specs=specs or [VMEM] * le...  10.7 us

profile of v3, /device:TPU:1, one launch (start us, length us, event | category | flops | bytes accessed | tf_op | source)
XLA Modules:
  0.0 82.0 jit_solution(12906536912728097347)
XLA Ops:
  0.6 2.4 %shard_map.148 = bf16[2560,128]{1,0:T(8,128)(2,1)} custom-call(s32[1]{0:T(128)} %bitcast.rank_ref, bf16[128,1024]{1,0:T(8,128)(2,1)} %values_ref.3, bf16[128,1024]{1,0:T(8,128)(2,1)} %gates_ref.3, f32[128,1024]{1,0:T(8,128)} %grad_ref.3, bf16[128,1024]{1,0:T(8,128)(2,1)} %filter_ref.1), custom_call_target="tpu_custom_call" | custom-call | tf_op jit(solution)/shard_map/pallas_call | solution.py:185
  3.0 0.0 copy-start.3
  3.0 0.0 copy-start.4
  3.1 0.0 copy-start.5
  3.1 0.0 copy-start.6
  3.1 0.0 copy-start.7
  3.1 0.0 copy-start.8
  3.1 0.0 copy-start.9
  3.1 0.0 copy-start.10
  3.1 39.3 %all_to_all.10 = bf16[256,5,2,128]{3,2,1,0:T(2,128)(2,1)S(1)} all-to-all(bf16[256,5,2,128]{3,2,1,0:T(2,128)(2,1)} %bitcast.10), channel_id=1, replica_groups=mesh['seq'=64,'chan'=4] {'chan','seq'}, dimensions={0} | all-to-all | bytes 1310720 | tf_op jit(solution)/shard_map/all_to_all | solution.py:197
  42.5 0.0 copy-done.3
  42.5 0.0 copy-done.4
  42.5 0.0 copy-done.5
  42.5 0.0 copy-done.6
  42.5 0.0 copy-done.7
  42.5 0.0 copy-done.8
  42.5 0.0 copy-done.9
  42.5 0.0 copy-done.10
  42.5 7.1 %shard_map.149 = bf16[3072,128]{1,0:T(8,128)(2,1)S(1)} custom-call(bf16[2560,128]{1,0:T(8,128)(2,1)S(1)} %bitcast.8, bf16[256,64]{1,0:T(8,128)(2,1)S(1)} %copy-done.7, bf16[128,128]{1,0:T(8,128)(2,1)S(1)} %copy-done.10, bf16[256,256]{1,0:T(8,128)(2,1)S(1)} %copy-done.6, bf16[256,256]{1,0:T(8,128)(2,1)S(1)} %copy-done.5, bf16[256,256]{1,0:T(8,128)(2,1)S(1)} %copy-done.4, ...), custom_call_target="tpu_custom_call" | custom-call | tf_op jit(solution)/shard_map/pallas_call | solution.py:185
  49.6 0.0 copy-start
  49.6 0.0 copy-start.1
  49.6 0.0 copy-start.2
  49.6 0.0 copy-start.11
  49.7 31.1 %all_to_all.11 = bf16[256,6,2,128]{3,2,1,0:T(2,128)(2,1)S(1)} all-to-all(bf16[256,6,2,128]{3,2,1,0:T(2,128)(2,1)S(1)} %bitcast.6), channel_id=1, replica_groups=mesh['seq'=64,'chan'=4] {'chan','seq'}, dimensions={0} | all-to-all | bytes 1572864 | tf_op jit(solution)/shard_map/all_to_all | solution.py:197
  80.8 0.0 copy-done
  80.8 0.0 copy-done.1
  80.8 0.0 copy-done.2
  80.8 0.0 copy-done.11
  80.8 1.2 %shard_map.150 = (bf16[128,1024]{1,0:T(8,128)(2,1)}, bf16[128,1024]{1,0:T(8,128)(2,1)}, f32[128,256]{1,0:T(8,128)}) custom-call(s32[1]{0:T(128)} %bitcast.rank_ref, bf16[128,1024]{1,0:T(8,128)(2,1)S(1)} %copy-done.1, bf16[128,1024]{1,0:T(8,128)(2,1)S(1)} %copy-done.2, f32[128,1024]{1,0:T(8,128)S(1)} %copy-done, f32[1,1024]{1,0:T(1,128)S(1)} %bitcast.9, ...), custom_call_target="tpu_custom_call" | custom-call | tf_op jit(solution)/shard_map/pallas_call | solution.py:185
Async XLA Ops:
  3.0 39.4 %copy-start.3 = (bf16[256,256]{1,0:T(8,128)(2,1)S(1)}, bf16[256,256]{1,0:T(8,128)(2,1)}, u32[]{:S(2)}) copy-start(bf16[256,256]{1,0:T(8,128)(2,1)} %constant.25.clone.inv_l) | copy-start | bytes 393220
  3.0 39.4 %copy-start.4 = (bf16[256,256]{1,0:T(8,128)(2,1)S(1)}, bf16[256,256]{1,0:T(8,128)(2,1)}, u32[]{:S(2)}) copy-start(bf16[256,256]{1,0:T(8,128)(2,1)} %constant.24.clone.inv_h) | copy-start | bytes 393220
  3.1 39.4 %copy-start.5 = (bf16[256,256]{1,0:T(8,128)(2,1)S(1)}, bf16[256,256]{1,0:T(8,128)(2,1)}, u32[]{:S(2)}) copy-start(bf16[256,256]{1,0:T(8,128)(2,1)} %constant.23.clone.fwd_l) | copy-start | bytes 393220
  3.1 39.4 %copy-start.6 = (bf16[256,256]{1,0:T(8,128)(2,1)S(1)}, bf16[256,256]{1,0:T(8,128)(2,1)}, u32[]{:S(2)}) copy-start(bf16[256,256]{1,0:T(8,128)(2,1)} %constant.22.clone.fwd_h) | copy-start | bytes 393220
  3.1 39.4 %copy-start.7 = (bf16[256,64]{1,0:T(8,128)(2,1)S(1)}, bf16[256,64]{1,0:T(8,128)(2,1)}, u32[]{:S(2)}) copy-start(bf16[256,64]{1,0:T(8,128)(2,1)} %constant.20.clone.enter_ref) | copy-start | bytes 98308
  3.1 39.4 %copy-start.8 = (f32[64,128]{1,0:T(8,128)S(1)}, f32[64,128]{1,0:T(8,128)}, u32[]{:S(2)}) copy-start(f32[64,128]{1,0:T(8,128)} %constant.27.clone.sin_ref) | copy-start | bytes 98308
  3.1 39.4 %copy-start.9 = (f32[64,128]{1,0:T(8,128)S(1)}, f32[64,128]{1,0:T(8,128)}, u32[]{:S(2)}) copy-start(f32[64,128]{1,0:T(8,128)} %constant.26.clone.cos_ref) | copy-start | bytes 98308
  3.1 39.4 %copy-start.10 = (bf16[128,128]{1,0:T(8,128)(2,1)S(1)}, bf16[128,128]{1,0:T(8,128)(2,1)}, u32[]{:S(2)}) copy-start(bf16[128,128]{1,0:T(8,128)(2,1)} %constant.21.clone.leave_ref) | copy-start | bytes 98308
  49.6 31.1 %copy-start = (f32[128,1024]{1,0:T(8,128)S(1)}, f32[128,1024]{1,0:T(8,128)}, u32[]{:S(2)}) copy-start(f32[128,1024]{1,0:T(8,128)} %grad_ref.3) | copy-start | bytes 1572868
  49.6 31.1 %copy-start.1 = (bf16[128,1024]{1,0:T(8,128)(2,1)S(1)}, bf16[128,1024]{1,0:T(8,128)(2,1)}, u32[]{:S(2)}) copy-start(bf16[128,1024]{1,0:T(8,128)(2,1)} %values_ref.3) | copy-start | bytes 786436
  49.6 31.1 %copy-start.2 = (bf16[128,1024]{1,0:T(8,128)(2,1)S(1)}, bf16[128,1024]{1,0:T(8,128)(2,1)}, u32[]{:S(2)}) copy-start(bf16[128,1024]{1,0:T(8,128)(2,1)} %gates_ref.3) | copy-start | bytes 786436
  49.6 31.1 %copy-start.11 = (f32[1024]{0:T(1024)S(1)}, f32[1024]{0:T(1024)}, u32[]{:S(2)}) copy-start(f32[1024]{0:T(1024)} %param.17) | copy-start | bytes 12292

commit v4 on v3

--- a/solution.py
+++ b/solution.py
@@ -12,8 +12,7 @@
 BF16 = jnp.bfloat16
 VMEM = pl.BlockSpec(memory_space=pltpu.VMEM)
 SHARE = 4
-SENT = 10
-BACK = 12
+LINES = 10
 WIDE = True
 
 
@@ -66,8 +65,8 @@
     return dot(x_high, high) + (dot(x_low, high) + dot(x_high, low))
 
 
-def pack_kernel(rank_ref, values_ref, gates_ref, grad_ref, filter_ref, out_ref, values, gates, grad, taps, flat, rows_ref, sems):
-    pairs = flat.shape[0] // SHARE
+def pack_kernel(rank_ref, values_ref, gates_ref, grad_ref, filter_ref, out_ref, values, gates, grad, taps, rows_ref, sems):
+    pairs = rows_ref.shape[0] // LINES
     copies = [
         pltpu.make_async_copy(src, dst, sems.at[k])
         for k, (src, dst) in enumerate(
@@ -77,21 +76,25 @@
     for copy in copies:
         copy.start()
 
-    def place(part, sources, start):
-        flat[...] = part.T
-        for k, source in enumerate(sources):
-            rows_ref[pl.ds(start + k, pairs, stride=SENT), :] = flat[
-                pl.ds(source, pairs, stride=SHARE), :
-            ]
+    def put(line, rows):
+        rows_ref[pl.ds(line, pairs, stride=LINES), :] = rows
+
+    def place(part, first):
+        turned = part.T
+        for q in range(SHARE):
+            put(first + q, turned[q * pairs : (q + 1) * pairs, :])
 
     copies[0].wait()
-    place(values[...].astype(F32), range(SHARE), 0)
+    place(values[...].astype(F32), 0)
     copies[1].wait()
-    place(taps[...].astype(F32), (rank_ref[0], rank_ref[0]), 2 * SHARE)
+    start = pl.multiple_of(rank_ref[0] * pairs, pairs)
+    own = taps[:, pl.ds(start, pairs)].astype(F32).T
+    for line in range(2 * SHARE, LINES):
+        put(line, own)
     copies[2].wait()
     copies[3].wait()
     gate_term = (grad[...] * gates[...].astype(F32)).astype(BF16).astype(F32)
-    place(gate_term, range(SHARE), SHARE)
+    place(gate_term, SHARE)
     out_ref[...] = rows_ref[...].astype(BF16)
 
 
@@ -99,12 +102,12 @@
     in_ref, enter_ref, leave_ref, fwd_h, fwd_l, inv_h, inv_l, cos_ref, sin_ref, out_ref, wide, result
 ):
     blocks, rows = cos_ref.shape
-    copies = in_ref.shape[0] // (blocks * SENT)
+    copies = in_ref.shape[0] // (blocks * LINES)
     cos_t, sin_t = cos_ref[...], sin_ref[...]
     wide[...] = in_ref[...].astype(F32)
 
     def spectrum(starts):
-        cols = [wide[pl.ds(start, blocks, stride=SENT), :] for start in starts]
+        cols = [wide[pl.ds(start, blocks, stride=LINES), :] for start in starts]
         mixed = dot(enter_ref[...], jnp.concatenate(cols, axis=1).astype(BF16))
         if WIDE:
             mixed = mixed[: 2 * blocks] + mixed[2 * blocks :]
@@ -138,12 +141,12 @@
 
     def put(block, first, cols):
         for c, col in enumerate(cols):
-            result[pl.ds(block * blocks * BACK + first + c, blocks, stride=BACK), :] = col
-
-    h_re, h_im = spectrum([c * blocks * SENT + 2 * SHARE for c in range(SHARE)])
+            result[pl.ds(block * blocks * LINES + first + c, blocks, stride=LINES), :] = col
+
+    h_re, h_im = spectrum([c * blocks * LINES + 2 * SHARE for c in range(SHARE)])
     f_re = f_im = None
     for j in range(copies):
-        base = j * blocks * SENT
+        base = j * blocks * LINES
         v_re, v_im = spectrum([base + c for c in range(SHARE)])
         put(j, 0, signal(h_re * v_re - h_im * v_im, h_re * v_im + h_im * v_re))
         g_re, g_im = spectrum([base + SHARE + c for c in range(SHARE)])
@@ -152,20 +155,22 @@
         f_re, f_im = (re, im) if j == 0 else (f_re + re, f_im + im)
     terms = signal(f_re, f_im)
     for j in range(copies):
-        put(j, 2 * SHARE, terms)
+        for line in range(2 * SHARE, LINES):
+            put(j, line, [terms[j]])
     out_ref[...] = result[...].astype(BF16)
 
 
 def finish_kernel(
-    rank_ref, values_ref, gates_ref, grad_ref, skip_ref, in_ref, value_out, gate_out, filter_out, wide, flat
+    values_ref, gates_ref, grad_ref, skip_ref, in_ref, value_out, gate_out, filter_out, wide, flat
 ):
     pairs = flat.shape[0] // SHARE
-    own = filter_out.shape[1]
     wide[...] = in_ref[...].astype(F32)
 
     def part(first):
-        for c in range(SHARE):
-            flat[pl.ds(c, pairs, stride=SHARE), :] = wide[pl.ds(first + c, pairs, stride=BACK), :]
+        for q in range(SHARE):
+            flat[q * pairs : (q + 1) * pairs, :] = wide[
+                pl.ds(first + q, pairs, stride=LINES), :
+            ]
         return flat[...].T
 
     grad = grad_ref[...]
@@ -173,12 +178,7 @@
     gate_out[...] = (grad * (part(0) + skip * values_ref[...].astype(F32))).astype(BF16)
     gate_term = (grad * gates_ref[...].astype(F32)).astype(BF16).astype(F32)
     value_out[...] = (part(SHARE) + skip * gate_term).astype(BF16)
-    start = rank_ref[0] * (own // SHARE * BACK) + 2 * SHARE
-    for c in range(SHARE):
-        flat[pl.ds(c, own // SHARE, stride=SHARE), :] = wide[
-            pl.ds(start + c, own // SHARE, stride=BACK), :
-        ]
-    filter_out[...] = flat[:own, :].T
+    filter_out[...] = wide[pl.ds(2 * SHARE, pairs, stride=LINES), :].T
 
 
 def call(kernel, out_shape, args, scratch, specs=None, limit=48):
@@ -200,13 +200,12 @@
 
 def transform(held, blocks):
     rows = held.shape[1]
-    back = held.shape[0] // SENT * BACK
     consts = tables(blocks, rows)
     return call(
         spectra_kernel,
-        jax.ShapeDtypeStruct((back, rows), BF16),
+        jax.ShapeDtypeStruct(held.shape, BF16),
         (held, *consts),
-        [pltpu.VMEM(held.shape, F32), pltpu.VMEM((back, rows), F32)],
+        [pltpu.VMEM(held.shape, F32), pltpu.VMEM(held.shape, F32)],
     )
 
 
@@ -219,15 +218,14 @@
     scalar = pl.BlockSpec(memory_space=pltpu.SMEM)
     sent = call(
         pack_kernel,
-        jax.ShapeDtypeStruct((pairs * SENT, rows), BF16),
+        jax.ShapeDtypeStruct((pairs * LINES, rows), BF16),
         (rank, values, gates, grad_out, filter_raw),
         [
             pltpu.VMEM((rows, width), BF16),
             pltpu.VMEM((rows, width), BF16),
             pltpu.VMEM((rows, width), F32),
             pltpu.VMEM((rows, width), BF16),
-            flat,
-            pltpu.VMEM((pairs * SENT, rows), F32),
+            pltpu.VMEM((pairs * LINES, rows), F32),
             pltpu.SemaphoreType.DMA((4,)),
         ],
         [scalar] + [pl.BlockSpec(memory_space=pltpu.HBM)] * 4,
@@ -238,9 +236,8 @@
     return call(
         finish_kernel,
         (shape, shape, jax.ShapeDtypeStruct((rows, width // lax.axis_size("chan")), F32)),
-        (rank, values, gates, grad_out, skip_gain[None, :], back),
+        (values, gates, grad_out, skip_gain[None, :], back),
         [pltpu.VMEM(back.shape, F32), flat],
-        [scalar] + [VMEM] * 5,
     )
 
 

time: 82.2 us -> 79.6 us (0.968)
  blocking collectives: 70.4 us -> 68 us
    all_to_all x2, blocking collectives: 70.4 us -> 68 us  [exchange(): lax.all_to_all(shaped, ('chan', 'seq'), split_axis=0, concat_axis=0, tile...]
where the time goes in v4:
time: 79.6 us; the launch traced here: 79.4 us
  blocking collectives  68 us (85%)
  Pallas kernels  10.5 us (13%)
  between operations  0.8 us (1%)
    all_to_all x2, blocking collectives, exchange(): lax.all_to_all(shaped, ('chan', 'seq'), split_axis=0, concat_axis=0, tile...  68 us
    pallas_call x3, Pallas kernels, call(): pl.pallas_call(kernel, out_shape=out_shape, in_specs=specs or [VMEM] * le...  10.5 us

profile of v4, /device:TPU:1, one launch (start us, length us, event | category | flops | bytes accessed | tf_op | source)
XLA Modules:
  0.0 79.4 jit_solution(17546512142066972462)
XLA Ops:
  0.6 2.3 %shard_map.148 = bf16[2560,128]{1,0:T(8,128)(2,1)} custom-call(s32[1]{0:T(128)} %bitcast.1.rank_ref, bf16[128,1024]{1,0:T(8,128)(2,1)} %values_ref.3, bf16[128,1024]{1,0:T(8,128)(2,1)} %gates_ref.3, f32[128,1024]{1,0:T(8,128)} %grad_ref.3, bf16[128,1024]{1,0:T(8,128)(2,1)} %filter_ref.1), custom_call_target="tpu_custom_call" | custom-call | tf_op jit(solution)/shard_map/pallas_call | solution.py:185
  3.0 0.0 copy-start.3
  3.0 0.0 copy-start.4
  3.0 0.0 copy-start.5
  3.0 0.0 copy-start.6
  3.0 0.0 copy-start.7
  3.0 0.0 copy-start.8
  3.1 0.0 copy-start.9
  3.1 0.0 copy-start.10
  3.1 39.3 %all_to_all.10 = bf16[256,5,2,128]{3,2,1,0:T(2,128)(2,1)S(1)} all-to-all(bf16[256,5,2,128]{3,2,1,0:T(2,128)(2,1)} %bitcast.10), channel_id=1, replica_groups=mesh['seq'=64,'chan'=4] {'chan','seq'}, dimensions={0} | all-to-all | bytes 1310720 | tf_op jit(solution)/shard_map/all_to_all | solution.py:197
  42.4 0.0 copy-done.3
  42.4 0.0 copy-done.4
  42.4 0.0 copy-done.5
  42.4 0.0 copy-done.6
  42.4 0.0 copy-done.7
  42.4 0.0 copy-done.8
  42.5 0.0 copy-done.9
  42.5 0.0 copy-done.10
  42.5 7.0 %shard_map.149 = bf16[2560,128]{1,0:T(8,128)(2,1)S(1)} custom-call(bf16[2560,128]{1,0:T(8,128)(2,1)S(1)} %bitcast.6, bf16[256,64]{1,0:T(8,128)(2,1)S(1)} %copy-done.7, bf16[128,128]{1,0:T(8,128)(2,1)S(1)} %copy-done.10, bf16[256,256]{1,0:T(8,128)(2,1)S(1)} %copy-done.6, bf16[256,256]{1,0:T(8,128)(2,1)S(1)} %copy-done.5, bf16[256,256]{1,0:T(8,128)(2,1)S(1)} %copy-done.4, ...), custom_call_target="tpu_custom_call" | custom-call | tf_op jit(solution)/shard_map/pallas_call | solution.py:185
  49.5 0.0 copy-start
  49.5 0.0 copy-start.1
  49.5 0.0 copy-start.2
  49.6 0.0 copy-start.11
  49.6 28.6 %all_to_all.11 = bf16[256,5,2,128]{3,2,1,0:T(2,128)(2,1)S(1)} all-to-all(bf16[256,5,2,128]{3,2,1,0:T(2,128)(2,1)S(1)} %bitcast.7), channel_id=1, replica_groups=mesh['seq'=64,'chan'=4] {'chan','seq'}, dimensions={0} | all-to-all | bytes 1310720 | tf_op jit(solution)/shard_map/all_to_all | solution.py:197
  78.2 0.0 copy-done
  78.2 0.0 copy-done.1
  78.2 0.0 copy-done.2
  78.2 0.0 copy-done.11
  78.2 1.1 %shard_map.150 = (bf16[128,1024]{1,0:T(8,128)(2,1)}, bf16[128,1024]{1,0:T(8,128)(2,1)}, f32[128,256]{1,0:T(8,128)}) custom-call(bf16[128,1024]{1,0:T(8,128)(2,1)S(1)} %copy-done.1, bf16[128,1024]{1,0:T(8,128)(2,1)S(1)} %copy-done.2, f32[128,1024]{1,0:T(8,128)S(1)} %copy-done, f32[1,1024]{1,0:T(1,128)S(1)} %bitcast.9, bf16[2560,128]{1,0:T(8,128)(2,1)S(1)} %bitcast.8), custom_call_target="tpu_custom_call" | custom-call | tf_op jit(solution)/shard_map/pallas_call | solution.py:185
Async XLA Ops:
  3.0 39.4 %copy-start.3 = (bf16[256,256]{1,0:T(8,128)(2,1)S(1)}, bf16[256,256]{1,0:T(8,128)(2,1)}, u32[]{:S(2)}) copy-start(bf16[256,256]{1,0:T(8,128)(2,1)} %constant.25.clone.inv_l) | copy-start | bytes 393220
  3.0 39.4 %copy-start.4 = (bf16[256,256]{1,0:T(8,128)(2,1)S(1)}, bf16[256,256]{1,0:T(8,128)(2,1)}, u32[]{:S(2)}) copy-start(bf16[256,256]{1,0:T(8,128)(2,1)} %constant.24.clone.inv_h) | copy-start | bytes 393220
  3.0 39.4 %copy-start.5 = (bf16[256,256]{1,0:T(8,128)(2,1)S(1)}, bf16[256,256]{1,0:T(8,128)(2,1)}, u32[]{:S(2)}) copy-start(bf16[256,256]{1,0:T(8,128)(2,1)} %constant.23.clone.fwd_l) | copy-start | bytes 393220
  3.0 39.4 %copy-start.6 = (bf16[256,256]{1,0:T(8,128)(2,1)S(1)}, bf16[256,256]{1,0:T(8,128)(2,1)}, u32[]{:S(2)}) copy-start(bf16[256,256]{1,0:T(8,128)(2,1)} %constant.22.clone.fwd_h) | copy-start | bytes 393220
  3.0 39.4 %copy-start.7 = (bf16[256,64]{1,0:T(8,128)(2,1)S(1)}, bf16[256,64]{1,0:T(8,128)(2,1)}, u32[]{:S(2)}) copy-start(bf16[256,64]{1,0:T(8,128)(2,1)} %constant.20.clone.enter_ref) | copy-start | bytes 98308
  3.0 39.4 %copy-start.8 = (f32[64,128]{1,0:T(8,128)S(1)}, f32[64,128]{1,0:T(8,128)}, u32[]{:S(2)}) copy-start(f32[64,128]{1,0:T(8,128)} %constant.27.clone.sin_ref) | copy-start | bytes 98308
  3.1 39.4 %copy-start.9 = (f32[64,128]{1,0:T(8,128)S(1)}, f32[64,128]{1,0:T(8,128)}, u32[]{:S(2)}) copy-start(f32[64,128]{1,0:T(8,128)} %constant.26.clone.cos_ref) | copy-start | bytes 98308
  3.1 39.4 %copy-start.10 = (bf16[128,128]{1,0:T(8,128)(2,1)S(1)}, bf16[128,128]{1,0:T(8,128)(2,1)}, u32[]{:S(2)}) copy-start(bf16[128,128]{1,0:T(8,128)(2,1)} %constant.21.clone.leave_ref) | copy-start | bytes 98308
  49.5 28.7 %copy-start = (f32[128,1024]{1,0:T(8,128)S(1)}, f32[128,1024]{1,0:T(8,128)}, u32[]{:S(2)}) copy-start(f32[128,1024]{1,0:T(8,128)} %grad_ref.3) | copy-start | bytes 1572868
  49.5 28.7 %copy-start.1 = (bf16[128,1024]{1,0:T(8,128)(2,1)S(1)}, bf16[128,1024]{1,0:T(8,128)(2,1)}, u32[]{:S(2)}) copy-start(bf16[128,1024]{1,0:T(8,128)(2,1)} %values_ref.3) | copy-start | bytes 786436
  49.5 28.7 %copy-start.2 = (bf16[128,1024]{1,0:T(8,128)(2,1)S(1)}, bf16[128,1024]{1,0:T(8,128)(2,1)}, u32[]{:S(2)}) copy-start(bf16[128,1024]{1,0:T(8,128)(2,1)} %gates_ref.3) | copy-start | bytes 786436
  49.6 28.7 %copy-start.11 = (f32[1024]{0:T(1024)S(1)}, f32[1024]{0:T(1024)}, u32[]{:S(2)}) copy-start(f32[1024]{0:T(1024)} %param.17) | copy-start | bytes 12292

commit v5 on v4

--- a/solution.py
+++ b/solution.py
@@ -12,8 +12,8 @@
 BF16 = jnp.bfloat16
 VMEM = pl.BlockSpec(memory_space=pltpu.VMEM)
 SHARE = 4
+PIECES = 4
 LINES = 10
-WIDE = True
 
 
 def split_pair(table):
@@ -34,16 +34,15 @@
     row_cos, row_sin = np.cos(row_angle), np.sin(row_angle)
     forward = np.block([[row_cos, -row_sin], [row_sin, row_cos]])
     inverse = np.block([[row_cos, row_sin], [-row_sin, row_cos]])
-    enter_pair = np.concatenate(split_pair(enter), axis=0)
+    enter_high, enter_low = split_pair(enter)
     leave_high, leave_low = split_pair(leave)
-    leave_pair = np.concatenate([leave_high, leave_low], axis=0)
-    if not WIDE:
-        enter_pair, leave_pair = enter_pair[: 2 * blocks], leave_pair[:blocks]
     return (
-        enter_pair,
-        leave_pair,
-        *split_pair(forward),
-        *split_pair(inverse),
+        np.concatenate([enter_high, enter_low], axis=1),
+        np.concatenate([leave_high, leave_low, leave_high], axis=1),
+        *(
+            np.concatenate([high, low, high], axis=0)
+            for high, low in (split_pair(forward), split_pair(inverse))
+        ),
         np.cos(turn).astype(np.float32),
         np.sin(turn).astype(np.float32),
     )
@@ -58,11 +57,15 @@
     return jnp.dot(a, b, preferred_element_type=F32)
 
 
-def dot_wide(x, high, low):
-    if not WIDE:
-        return dot(x.astype(BF16), high)
-    x_high, x_low = split_value(x)
-    return dot(x_high, high) + (dot(x_low, high) + dot(x_high, low))
+def triple(x, axis):
+    high, low = split_value(x)
+    return jnp.concatenate([high, high, low], axis=axis)
+
+
+def dot_rows(x, table):
+    size = x.shape[0] // PIECES
+    parts = [dot(triple(x[k * size : (k + 1) * size], 1), table) for k in range(PIECES)]
+    return jnp.concatenate(parts, axis=0)
 
 
 def pack_kernel(rank_ref, values_ref, gates_ref, grad_ref, filter_ref, out_ref, values, gates, grad, taps, rows_ref, sems):
@@ -99,7 +102,7 @@
 
 
 def spectra_kernel(
-    in_ref, enter_ref, leave_ref, fwd_h, fwd_l, inv_h, inv_l, cos_ref, sin_ref, out_ref, wide, result
+    in_ref, enter_ref, leave_ref, forward_ref, inverse_ref, cos_ref, sin_ref, out_ref, wide, result
 ):
     blocks, rows = cos_ref.shape
     copies = in_ref.shape[0] // (blocks * LINES)
@@ -108,55 +111,56 @@
 
     def spectrum(starts):
         cols = [wide[pl.ds(start, blocks, stride=LINES), :] for start in starts]
-        mixed = dot(enter_ref[...], jnp.concatenate(cols, axis=1).astype(BF16))
-        if WIDE:
-            mixed = mixed[: 2 * blocks] + mixed[2 * blocks :]
+        joined = jnp.concatenate(cols, axis=1).astype(BF16)
+        mixed = dot(enter_ref[...], jnp.concatenate([joined, joined], axis=0))
         turned = []
-        for c in range(SHARE):
+        for c in range(len(starts)):
             re = mixed[:blocks, c * rows : (c + 1) * rows]
             im = mixed[blocks:, c * rows : (c + 1) * rows]
             turned.append(
                 jnp.concatenate([re * cos_t + im * sin_t, im * cos_t - re * sin_t], axis=1)
             )
-        full = dot_wide(jnp.concatenate(turned, axis=0), fwd_h[...], fwd_l[...])
+        full = dot_rows(jnp.concatenate(turned, axis=0), forward_ref[...])
         return full[:, :rows], full[:, rows:]
 
     def signal(re, im):
-        full = dot_wide(jnp.concatenate([re, im], axis=1), inv_h[...], inv_l[...])
+        full = dot_rows(jnp.concatenate([re, im], axis=1), inverse_ref[...])
         cols = []
-        for c in range(SHARE):
+        for c in range(full.shape[0] // blocks):
             re = full[c * blocks : (c + 1) * blocks, :rows]
             im = full[c * blocks : (c + 1) * blocks, rows:]
             cols.append(
                 jnp.concatenate([re * cos_t - im * sin_t, re * sin_t + im * cos_t], axis=0)
             )
-        joined = jnp.concatenate(cols, axis=1)
-        if not WIDE:
-            mixed = dot(leave_ref[...], joined.astype(BF16))
-        else:
-            high, low = split_value(joined)
-            pair = dot(leave_ref[...], high)
-            mixed = pair[:blocks] + (pair[blocks:] + dot(leave_ref[:blocks, :], low))
-        return [mixed[:, c * rows : (c + 1) * rows] for c in range(SHARE)]
-
-    def put(block, first, cols):
-        for c, col in enumerate(cols):
-            result[pl.ds(block * blocks * LINES + first + c, blocks, stride=LINES), :] = col
-
-    h_re, h_im = spectrum([c * blocks * LINES + 2 * SHARE for c in range(SHARE)])
-    f_re = f_im = None
-    for j in range(copies):
-        base = j * blocks * LINES
-        v_re, v_im = spectrum([base + c for c in range(SHARE)])
-        put(j, 0, signal(h_re * v_re - h_im * v_im, h_re * v_im + h_im * v_re))
-        g_re, g_im = spectrum([base + SHARE + c for c in range(SHARE)])
-        put(j, SHARE, signal(h_re * g_re + h_im * g_im, h_re * g_im - h_im * g_re))
-        re, im = v_re * g_re + v_im * g_im, v_re * g_im - v_im * g_re
-        f_re, f_im = (re, im) if j == 0 else (f_re + re, f_im + im)
-    terms = signal(f_re, f_im)
-    for j in range(copies):
+        mixed = dot(leave_ref[...], triple(jnp.concatenate(cols, axis=1), 0))
+        return [mixed[:, c * rows : (c + 1) * rows] for c in range(len(cols))]
+
+    def put(block, line, col):
+        result[pl.ds(block * blocks * LINES + line, blocks, stride=LINES), :] = col
+
+    pairs = [(j, q) for j in range(copies) for q in range(SHARE)]
+    size, part = len(pairs) * blocks, SHARE * blocks
+    re, im = spectrum(
+        [j * blocks * LINES + q for j, q in pairs]
+        + [j * blocks * LINES + SHARE + q for j, q in pairs]
+        + [q * blocks * LINES + 2 * SHARE for q in range(SHARE)]
+    )
+    v_re, v_im, g_re, g_im = re[:size], im[:size], re[size : 2 * size], im[size : 2 * size]
+    h_re = jnp.concatenate([re[2 * size :]] * copies, axis=0)
+    h_im = jnp.concatenate([im[2 * size :]] * copies, axis=0)
+    f_re, f_im = v_re * g_re + v_im * g_im, v_re * g_im - v_im * g_re
+    f_re = sum(f_re[j * part : (j + 1) * part] for j in range(copies))
+    f_im = sum(f_im[j * part : (j + 1) * part] for j in range(copies))
+    cols = signal(
+        jnp.concatenate([h_re * v_re - h_im * v_im, h_re * g_re + h_im * g_im, f_re], axis=0),
+        jnp.concatenate([h_re * v_im + h_im * v_re, h_re * g_im - h_im * g_re, f_im], axis=0),
+    )
+    for k, (j, q) in enumerate(pairs):
+        put(j, q, cols[k])
+        put(j, SHARE + q, cols[len(pairs) + k])
+    for j in range(SHARE):
         for line in range(2 * SHARE, LINES):
-            put(j, line, [terms[j]])
+            put(j, line, cols[2 * len(pairs) + j])
     out_ref[...] = result[...].astype(BF16)
 
 

time: 79.6 us -> 75.8 us (0.952)
  Pallas kernels: 10.5 us -> 6.81 us
    pallas_call x3, Pallas kernels: 10.5 us -> 6.81 us  [call(): pl.pallas_call(kernel, out_shape=out_shape, in_specs=specs or [VMEM] * le...]
where the time goes in v5:
time: 75.8 us; the launch traced here: 75.6 us
  blocking collectives  68 us (90%)
  Pallas kernels  6.81 us (9%)
  between operations  0.77 us (1%)
    all_to_all x2, blocking collectives, exchange(): lax.all_to_all(shaped, ('chan', 'seq'), split_axis=0, concat_axis=0, tile...  68 us
    pallas_call x3, Pallas kernels, call(): pl.pallas_call(kernel, out_shape=out_shape, in_specs=specs or [VMEM] * le...  6.81 us

profile of v5, /device:TPU:1, one launch (start us, length us, event | category | flops | bytes accessed | tf_op | source)
XLA Modules:
  0.0 75.6 jit_solution(13439866622505397547)
XLA Ops:
  0.6 2.3 %shard_map.130 = bf16[2560,128]{1,0:T(8,128)(2,1)} custom-call(s32[1]{0:T(128)} %bitcast.1.rank_ref, bf16[128,1024]{1,0:T(8,128)(2,1)} %values_ref.3, bf16[128,1024]{1,0:T(8,128)(2,1)} %gates_ref.3, f32[128,1024]{1,0:T(8,128)} %grad_ref.3, bf16[128,1024]{1,0:T(8,128)(2,1)} %filter_ref.1), custom_call_target="tpu_custom_call" | custom-call | tf_op jit(solution)/shard_map/pallas_call | solution.py:189
  3.0 0.0 copy-start.3
  3.0 0.0 copy-start.4
  3.0 0.0 copy-start.5
  3.0 0.0 copy-start.6
  3.0 0.0 copy-start.7
  3.0 0.0 copy-start.8
  3.1 39.3 %all_to_all.10 = bf16[256,5,2,128]{3,2,1,0:T(2,128)(2,1)S(1)} all-to-all(bf16[256,5,2,128]{3,2,1,0:T(2,128)(2,1)} %bitcast.10), channel_id=1, replica_groups=mesh['seq'=64,'chan'=4] {'chan','seq'}, dimensions={0} | all-to-all | bytes 1310720 | tf_op jit(solution)/shard_map/all_to_all | solution.py:201
  42.4 0.0 copy-done.3
  42.4 0.0 copy-done.4
  42.4 0.0 copy-done.5
  42.4 0.0 copy-done.6
  42.4 0.0 copy-done.7
  42.4 0.0 copy-done.8
  42.4 3.3 %shard_map.131 = bf16[2560,128]{1,0:T(8,128)(2,1)S(1)} custom-call(bf16[2560,128]{1,0:T(8,128)(2,1)S(1)} %bitcast.7, bf16[128,128]{1,0:T(8,128)(2,1)S(1)} %copy-done.8, bf16[64,384]{1,0:T(8,128)(2,1)S(1)} %copy-done.5, bf16[768,256]{1,0:T(8,128)(2,1)S(1)} %copy-done.4, bf16[768,256]{1,0:T(8,128)(2,1)S(1)} %copy-done.3, f32[64,128]{1,0:T(8,128)S(1)} %copy-done.7, ...), custom_call_target="tpu_custom_call" | custom-call | tf_op jit(solution)/shard_map/pallas_call | solution.py:189
  45.8 0.0 copy-start
  45.8 0.0 copy-start.1
  45.8 0.0 copy-start.2
  45.8 0.0 copy-start.9
  45.8 28.6 %all_to_all.11 = bf16[256,5,2,128]{3,2,1,0:T(2,128)(2,1)S(1)} all-to-all(bf16[256,5,2,128]{3,2,1,0:T(2,128)(2,1)S(1)} %bitcast.8), channel_id=1, replica_groups=mesh['seq'=64,'chan'=4] {'chan','seq'}, dimensions={0} | all-to-all | bytes 1310720 | tf_op jit(solution)/shard_map/all_to_all | solution.py:201
  74.5 0.0 copy-done
  74.5 0.0 copy-done.1
  74.5 0.0 copy-done.2
  74.5 0.0 copy-done.9
  74.5 1.1 %shard_map.132 = (bf16[128,1024]{1,0:T(8,128)(2,1)}, bf16[128,1024]{1,0:T(8,128)(2,1)}, f32[128,256]{1,0:T(8,128)}) custom-call(bf16[128,1024]{1,0:T(8,128)(2,1)S(1)} %copy-done.1, bf16[128,1024]{1,0:T(8,128)(2,1)S(1)} %copy-done.2, f32[128,1024]{1,0:T(8,128)S(1)} %copy-done, f32[1,1024]{1,0:T(1,128)S(1)} %bitcast.9, bf16[2560,128]{1,0:T(8,128)(2,1)S(1)} %bitcast.6), custom_call_target="tpu_custom_call" | custom-call | tf_op jit(solution)/shard_map/pallas_call | solution.py:189
Async XLA Ops:
  3.0 39.4 %copy-start.3 = (bf16[768,256]{1,0:T(8,128)(2,1)S(1)}, bf16[768,256]{1,0:T(8,128)(2,1)}, u32[]{:S(2)}) copy-start(bf16[768,256]{1,0:T(8,128)(2,1)} %constant.19.clone.inverse_ref) | copy-start | bytes 1179652
  3.0 39.4 %copy-start.4 = (bf16[768,256]{1,0:T(8,128)(2,1)S(1)}, bf16[768,256]{1,0:T(8,128)(2,1)}, u32[]{:S(2)}) copy-start(bf16[768,256]{1,0:T(8,128)(2,1)} %constant.18.clone.forward_ref) | copy-start | bytes 1179652
  3.0 39.4 %copy-start.5 = (bf16[64,384]{1,0:T(8,128)(2,1)S(1)}, bf16[64,384]{1,0:T(8,128)(2,1)}, u32[]{:S(2)}) copy-start(bf16[64,384]{1,0:T(8,128)(2,1)} %constant.17.clone.leave_ref) | copy-start | bytes 147460
  3.0 39.4 %copy-start.6 = (f32[64,128]{1,0:T(8,128)S(1)}, f32[64,128]{1,0:T(8,128)}, u32[]{:S(2)}) copy-start(f32[64,128]{1,0:T(8,128)} %constant.21.clone.sin_ref) | copy-start | bytes 98308
  3.0 39.4 %copy-start.7 = (f32[64,128]{1,0:T(8,128)S(1)}, f32[64,128]{1,0:T(8,128)}, u32[]{:S(2)}) copy-start(f32[64,128]{1,0:T(8,128)} %constant.20.clone.cos_ref) | copy-start | bytes 98308
  3.0 39.4 %copy-start.8 = (bf16[128,128]{1,0:T(8,128)(2,1)S(1)}, bf16[128,128]{1,0:T(8,128)(2,1)}, u32[]{:S(2)}) copy-start(bf16[128,128]{1,0:T(8,128)(2,1)} %constant.16.clone.enter_ref) | copy-start | bytes 98308
  45.8 28.7 %copy-start = (f32[128,1024]{1,0:T(8,128)S(1)}, f32[128,1024]{1,0:T(8,128)}, u32[]{:S(2)}) copy-start(f32[128,1024]{1,0:T(8,128)} %grad_ref.3) | copy-start | bytes 1572868
  45.8 28.7 %copy-start.1 = (bf16[128,1024]{1,0:T(8,128)(2,1)S(1)}, bf16[128,1024]{1,0:T(8,128)(2,1)}, u32[]{:S(2)}) copy-start(bf16[128,1024]{1,0:T(8,128)(2,1)} %values_ref.3) | copy-start | bytes 786436
  45.8 28.7 %copy-start.2 = (bf16[128,1024]{1,0:T(8,128)(2,1)S(1)}, bf16[128,1024]{1,0:T(8,128)(2,1)}, u32[]{:S(2)}) copy-start(bf16[128,1024]{1,0:T(8,128)(2,1)} %gates_ref.3) | copy-start | bytes 786436
  45.8 28.7 %copy-start.9 = (f32[1024]{0:T(1024)S(1)}, f32[1024]{0:T(1024)}, u32[]{:S(2)}) copy-start(f32[1024]{0:T(1024)} %param.15) | copy-start | bytes 12292

commit v6 on v5

--- a/solution.py
+++ b/solution.py
@@ -69,7 +69,7 @@
 
 
 def pack_kernel(rank_ref, values_ref, gates_ref, grad_ref, filter_ref, out_ref, values, gates, grad, taps, rows_ref, sems):
-    pairs = rows_ref.shape[0] // LINES
+    pairs = out_ref.shape[0] // LINES
     copies = [
         pltpu.make_async_copy(src, dst, sems.at[k])
         for k, (src, dst) in enumerate(
@@ -98,7 +98,7 @@
     copies[3].wait()
     gate_term = (grad[...] * gates[...].astype(F32)).astype(BF16).astype(F32)
     place(gate_term, SHARE)
-    out_ref[...] = rows_ref[...].astype(BF16)
+    out_ref[...] = rows_ref[: out_ref.shape[0], :].astype(BF16)
 
 
 def spectra_kernel(
@@ -107,7 +107,7 @@
     blocks, rows = cos_ref.shape
     copies = in_ref.shape[0] // (blocks * LINES)
     cos_t, sin_t = cos_ref[...], sin_ref[...]
-    wide[...] = in_ref[...].astype(F32)
+    wide[: in_ref.shape[0], :] = in_ref[...].astype(F32)
 
     def spectrum(starts):
         cols = [wide[pl.ds(start, blocks, stride=LINES), :] for start in starts]
@@ -161,14 +161,14 @@
     for j in range(SHARE):
         for line in range(2 * SHARE, LINES):
             put(j, line, cols[2 * len(pairs) + j])
-    out_ref[...] = result[...].astype(BF16)
+    out_ref[...] = result[: out_ref.shape[0], :].astype(BF16)
 
 
 def finish_kernel(
     values_ref, gates_ref, grad_ref, skip_ref, in_ref, value_out, gate_out, filter_out, wide, flat
 ):
     pairs = flat.shape[0] // SHARE
-    wide[...] = in_ref[...].astype(F32)
+    wide[: in_ref.shape[0], :] = in_ref[...].astype(F32)
 
     def part(first):
         for q in range(SHARE):
@@ -196,6 +196,10 @@
     )(*args)
 
 
+def spare(x):
+    return pltpu.VMEM((x.shape[0] + 16, x.shape[1]), F32)
+
+
 def exchange(x):
     shaped = x.reshape(lax.axis_size("chan") * lax.axis_size("seq"), -1, 2, x.shape[1])
     moved = lax.all_to_all(shaped, ("chan", "seq"), split_axis=0, concat_axis=0, tiled=True)
@@ -209,7 +213,7 @@
         spectra_kernel,
         jax.ShapeDtypeStruct(held.shape, BF16),
         (held, *consts),
-        [pltpu.VMEM(held.shape, F32), pltpu.VMEM(held.shape, F32)],
+        [spare(held), spare(held)],
     )
 
 
@@ -220,16 +224,17 @@
     rank = lax.axis_index("chan").astype(jnp.int32).reshape(1)
     flat = pltpu.VMEM((width, rows), F32)
     scalar = pl.BlockSpec(memory_space=pltpu.SMEM)
+    sent = jax.ShapeDtypeStruct((pairs * LINES, rows), BF16)
     sent = call(
         pack_kernel,
-        jax.ShapeDtypeStruct((pairs * LINES, rows), BF16),
+        sent,
         (rank, values, gates, grad_out, filter_raw),
         [
             pltpu.VMEM((rows, width), BF16),
             pltpu.VMEM((rows, width), BF16),
             pltpu.VMEM((rows, width), F32),
             pltpu.VMEM((rows, width), BF16),
-            pltpu.VMEM((pairs * LINES, rows), F32),
+            spare(sent),
             pltpu.SemaphoreType.DMA((4,)),
         ],
         [scalar] + [pl.BlockSpec(memory_space=pltpu.HBM)] * 4,
@@ -241,7 +246,7 @@
         finish_kernel,
         (shape, shape, jax.ShapeDtypeStruct((rows, width // lax.axis_size("chan")), F32)),
         (values, gates, grad_out, skip_gain[None, :], back),
-        [pltpu.VMEM(back.shape, F32), flat],
+        [spare(back), flat],
     )
 
 

time: 75.8 us -> 75.8 us (level)
  no operation moved by 1% of the time
where the time goes in v6:
time: 75.8 us; the launch traced here: 75.6 us
  blocking collectives  68 us (90%)
  Pallas kernels  6.81 us (9%)
  between operations  0.77 us (1%)
    all_to_all x2, blocking collectives, exchange(): lax.all_to_all(shaped, ('chan', 'seq'), split_axis=0, concat_axis=0, tile...  68 us
    pallas_call x3, Pallas kernels, call(): pl.pallas_call(kernel, out_shape=out_shape, in_specs=specs or [VMEM] * le...  6.81 us

profile of v6, /device:TPU:1, one launch (start us, length us, event | category | flops | bytes accessed | tf_op | source)
XLA Modules:
  0.0 75.6 jit_solution(13613787672504572978)
XLA Ops:
  0.6 2.3 %shard_map.130 = bf16[2560,128]{1,0:T(8,128)(2,1)} custom-call(s32[1]{0:T(128)} %bitcast.1.rank_ref, bf16[128,1024]{1,0:T(8,128)(2,1)} %values_ref.3, bf16[128,1024]{1,0:T(8,128)(2,1)} %gates_ref.3, f32[128,1024]{1,0:T(8,128)} %grad_ref.3, bf16[128,1024]{1,0:T(8,128)(2,1)} %filter_ref.1), custom_call_target="tpu_custom_call" | custom-call | tf_op jit(solution)/shard_map/pallas_call | solution.py:189
  3.0 0.0 copy-start.3
  3.0 0.0 copy-start.4
  3.0 0.0 copy-start.5
  3.0 0.0 copy-start.6
  3.0 0.0 copy-start.7
  3.0 0.0 copy-start.8
  3.1 39.3 %all_to_all.10 = bf16[256,5,2,128]{3,2,1,0:T(2,128)(2,1)S(1)} all-to-all(bf16[256,5,2,128]{3,2,1,0:T(2,128)(2,1)} %bitcast.10), channel_id=1, replica_groups=mesh['seq'=64,'chan'=4] {'chan','seq'}, dimensions={0} | all-to-all | bytes 1310720 | tf_op jit(solution)/shard_map/all_to_all | solution.py:205
  42.4 0.0 copy-done.3
  42.4 0.0 copy-done.4
  42.4 0.0 copy-done.5
  42.4 0.0 copy-done.6
  42.4 0.0 copy-done.7
  42.4 0.0 copy-done.8
  42.4 3.3 %shard_map.131 = bf16[2560,128]{1,0:T(8,128)(2,1)S(1)} custom-call(bf16[2560,128]{1,0:T(8,128)(2,1)S(1)} %bitcast.7, bf16[128,128]{1,0:T(8,128)(2,1)S(1)} %copy-done.8, bf16[64,384]{1,0:T(8,128)(2,1)S(1)} %copy-done.5, bf16[768,256]{1,0:T(8,128)(2,1)S(1)} %copy-done.4, bf16[768,256]{1,0:T(8,128)(2,1)S(1)} %copy-done.3, f32[64,128]{1,0:T(8,128)S(1)} %copy-done.7, ...), custom_call_target="tpu_custom_call" | custom-call | tf_op jit(solution)/shard_map/pallas_call | solution.py:189
  45.8 0.0 copy-start
  45.8 0.0 copy-start.1
  45.8 0.0 copy-start.2
  45.8 0.0 copy-start.9
  45.8 28.6 %all_to_all.11 = bf16[256,5,2,128]{3,2,1,0:T(2,128)(2,1)S(1)} all-to-all(bf16[256,5,2,128]{3,2,1,0:T(2,128)(2,1)S(1)} %bitcast.8), channel_id=1, replica_groups=mesh['seq'=64,'chan'=4] {'chan','seq'}, dimensions={0} | all-to-all | bytes 1310720 | tf_op jit(solution)/shard_map/all_to_all | solution.py:205
  74.5 0.0 copy-done
  74.5 0.0 copy-done.1
  74.5 0.0 copy-done.2
  74.5 0.0 copy-done.9
  74.5 1.1 %shard_map.132 = (bf16[128,1024]{1,0:T(8,128)(2,1)}, bf16[128,1024]{1,0:T(8,128)(2,1)}, f32[128,256]{1,0:T(8,128)}) custom-call(bf16[128,1024]{1,0:T(8,128)(2,1)S(1)} %copy-done.1, bf16[128,1024]{1,0:T(8,128)(2,1)S(1)} %copy-done.2, f32[128,1024]{1,0:T(8,128)S(1)} %copy-done, f32[1,1024]{1,0:T(1,128)S(1)} %bitcast.9, bf16[2560,128]{1,0:T(8,128)(2,1)S(1)} %bitcast.6), custom_call_target="tpu_custom_call" | custom-call | tf_op jit(solution)/shard_map/pallas_call | solution.py:189
Async XLA Ops:
  3.0 39.4 %copy-start.3 = (bf16[768,256]{1,0:T(8,128)(2,1)S(1)}, bf16[768,256]{1,0:T(8,128)(2,1)}, u32[]{:S(2)}) copy-start(bf16[768,256]{1,0:T(8,128)(2,1)} %constant.19.clone.inverse_ref) | copy-start | bytes 1179652
  3.0 39.4 %copy-start.4 = (bf16[768,256]{1,0:T(8,128)(2,1)S(1)}, bf16[768,256]{1,0:T(8,128)(2,1)}, u32[]{:S(2)}) copy-start(bf16[768,256]{1,0:T(8,128)(2,1)} %constant.18.clone.forward_ref) | copy-start | bytes 1179652
  3.0 39.4 %copy-start.5 = (bf16[64,384]{1,0:T(8,128)(2,1)S(1)}, bf16[64,384]{1,0:T(8,128)(2,1)}, u32[]{:S(2)}) copy-start(bf16[64,384]{1,0:T(8,128)(2,1)} %constant.17.clone.leave_ref) | copy-start | bytes 147460
  3.0 39.4 %copy-start.6 = (f32[64,128]{1,0:T(8,128)S(1)}, f32[64,128]{1,0:T(8,128)}, u32[]{:S(2)}) copy-start(f32[64,128]{1,0:T(8,128)} %constant.21.clone.sin_ref) | copy-start | bytes 98308
  3.0 39.4 %copy-start.7 = (f32[64,128]{1,0:T(8,128)S(1)}, f32[64,128]{1,0:T(8,128)}, u32[]{:S(2)}) copy-start(f32[64,128]{1,0:T(8,128)} %constant.20.clone.cos_ref) | copy-start | bytes 98308
  3.0 39.4 %copy-start.8 = (bf16[128,128]{1,0:T(8,128)(2,1)S(1)}, bf16[128,128]{1,0:T(8,128)(2,1)}, u32[]{:S(2)}) copy-start(bf16[128,128]{1,0:T(8,128)(2,1)} %constant.16.clone.enter_ref) | copy-start | bytes 98308
  45.8 28.7 %copy-start = (f32[128,1024]{1,0:T(8,128)S(1)}, f32[128,1024]{1,0:T(8,128)}, u32[]{:S(2)}) copy-start(f32[128,1024]{1,0:T(8,128)} %grad_ref.3) | copy-start | bytes 1572868
  45.8 28.7 %copy-start.1 = (bf16[128,1024]{1,0:T(8,128)(2,1)S(1)}, bf16[128,1024]{1,0:T(8,128)(2,1)}, u32[]{:S(2)}) copy-start(bf16[128,1024]{1,0:T(8,128)(2,1)} %values_ref.3) | copy-start | bytes 786436
  45.8 28.7 %copy-start.2 = (bf16[128,1024]{1,0:T(8,128)(2,1)S(1)}, bf16[128,1024]{1,0:T(8,128)(2,1)}, u32[]{:S(2)}) copy-start(bf16[128,1024]{1,0:T(8,128)(2,1)} %gates_ref.3) | copy-start | bytes 786436
  45.8 28.7 %copy-start.9 = (f32[1024]{0:T(1024)S(1)}, f32[1024]{0:T(1024)}, u32[]{:S(2)}) copy-start(f32[1024]{0:T(1024)} %param.15) | copy-start | bytes 12292

commit v7 on v6

--- a/solution.py
+++ b/solution.py
@@ -38,7 +38,7 @@
     leave_high, leave_low = split_pair(leave)
     return (
         np.concatenate([enter_high, enter_low], axis=1),
-        np.concatenate([leave_high, leave_low, leave_high], axis=1),
+        np.block([[leave_high, leave_high], [leave_low, np.zeros_like(leave_low)]]),
         *(
             np.concatenate([high, low, high], axis=0)
             for high, low in (split_pair(forward), split_pair(inverse))
@@ -110,30 +110,63 @@
     wide[: in_ref.shape[0], :] = in_ref[...].astype(F32)
 
     def spectrum(starts):
-        cols = [wide[pl.ds(start, blocks, stride=LINES), :] for start in starts]
-        joined = jnp.concatenate(cols, axis=1).astype(BF16)
-        mixed = dot(enter_ref[...], jnp.concatenate([joined, joined], axis=0))
-        turned = []
-        for c in range(len(starts)):
-            re = mixed[:blocks, c * rows : (c + 1) * rows]
-            im = mixed[blocks:, c * rows : (c + 1) * rows]
-            turned.append(
-                jnp.concatenate([re * cos_t + im * sin_t, im * cos_t - re * sin_t], axis=1)
-            )
-        full = dot_rows(jnp.concatenate(turned, axis=0), forward_ref[...])
+        table = forward_ref[...]
+        step = len(starts) // PIECES
+
+        def turn(first):
+            cols = [wide[pl.ds(start, blocks, stride=LINES), :] for start in starts[first : first + step]]
+            joined = jnp.concatenate(cols, axis=1).astype(BF16)
+            mixed = dot(enter_ref[...], jnp.concatenate([joined, joined], axis=0))
+            turned = []
+            for c in range(step):
+                re = mixed[:blocks, c * rows : (c + 1) * rows]
+                im = mixed[blocks:, c * rows : (c + 1) * rows]
+                turned.append(
+                    jnp.concatenate([re * cos_t + im * sin_t, im * cos_t - re * sin_t], axis=1)
+                )
+            return triple(jnp.concatenate(turned, axis=0), 1)
+
+        full = []
+        ready = turn(0)
+        for first in range(0, len(starts), step):
+            ahead = turn(first + step) if first + step < len(starts) else None
+            full.append(dot(ready, table))
+            ready = ahead
+        full = jnp.concatenate(full, axis=0)
         return full[:, :rows], full[:, rows:]
 
     def signal(re, im):
-        full = dot_rows(jnp.concatenate([re, im], axis=1), inverse_ref[...])
-        cols = []
-        for c in range(full.shape[0] // blocks):
-            re = full[c * blocks : (c + 1) * blocks, :rows]
-            im = full[c * blocks : (c + 1) * blocks, rows:]
-            cols.append(
-                jnp.concatenate([re * cos_t - im * sin_t, re * sin_t + im * cos_t], axis=0)
-            )
-        mixed = dot(leave_ref[...], triple(jnp.concatenate(cols, axis=1), 0))
-        return [mixed[:, c * rows : (c + 1) * rows] for c in range(len(cols))]
+        table = inverse_ref[...]
+        size = re.shape[0] // 4
+        starts = list(range(0, re.shape[0], size))
+
+        def product(k):
+            return dot(triple(jnp.concatenate([re[k : k + size], im[k : k + size]], axis=1), 1), table)
+
+        def turn(full):
+            cols = []
+            for c in range(0, size, blocks):
+                x, y = full[c : c + blocks, :rows], full[c : c + blocks, rows:]
+                cols.append(jnp.concatenate([x * cos_t - y * sin_t, x * sin_t + y * cos_t], axis=0))
+            return jnp.concatenate(split_value(jnp.concatenate(cols, axis=1)), axis=0)
+
+        waiting, done = [], []
+
+        def leave(x):
+            both = dot(leave_ref[...], x)
+            mixed = both[:blocks] + both[blocks:]
+            return [mixed[:, c : c + rows] for c in range(0, mixed.shape[1], rows)]
+
+        held = []
+        for k in starts:
+            waiting.append(product(k))
+            if len(waiting) > 1:
+                held.append(turn(waiting.pop(0)))
+        while waiting:
+            held.append(turn(waiting.pop(0)))
+        for x in held:
+            done += leave(x)
+        return done
 
     def put(block, line, col):
         result[pl.ds(block * blocks * LINES + line, blocks, stride=LINES), :] = col

time: 75.8 us -> 75.6 us (level)
  no operation moved by 1% of the time
where the time goes in v7:
time: 75.6 us; the launch traced here: 75.4 us
  blocking collectives  68 us (90%)
  Pallas kernels  6.64 us (9%)
  between operations  0.77 us (1%)
    all_to_all x2, blocking collectives, exchange(): lax.all_to_all(shaped, ('chan', 'seq'), split_axis=0, concat_axis=0, tile...  68 us
    pallas_call x3, Pallas kernels, call(): pl.pallas_call(kernel, out_shape=out_shape, in_specs=specs or [VMEM] * le...  6.64 us

profile of v7, /device:TPU:1, one launch (start us, length us, event | category | flops | bytes accessed | tf_op | source)
XLA Modules:
  0.0 75.4 jit_solution(18379367978875261314)
XLA Ops:
  0.6 2.3 %shard_map.130 = bf16[2560,128]{1,0:T(8,128)(2,1)} custom-call(s32[1]{0:T(128)} %bitcast.1.rank_ref, bf16[128,1024]{1,0:T(8,128)(2,1)} %values_ref.3, bf16[128,1024]{1,0:T(8,128)(2,1)} %gates_ref.3, f32[128,1024]{1,0:T(8,128)} %grad_ref.3, bf16[128,1024]{1,0:T(8,128)(2,1)} %filter_ref.1), custom_call_target="tpu_custom_call" | custom-call | tf_op jit(solution)/shard_map/pallas_call | solution.py:222
  3.0 0.0 copy-start.3
  3.0 0.0 copy-start.4
  3.0 0.0 copy-start.5
  3.0 0.0 copy-start.6
  3.0 0.0 copy-start.7
  3.0 0.0 copy-start.8
  3.1 39.3 %all_to_all.10 = bf16[256,5,2,128]{3,2,1,0:T(2,128)(2,1)S(1)} all-to-all(bf16[256,5,2,128]{3,2,1,0:T(2,128)(2,1)} %bitcast.10), channel_id=1, replica_groups=mesh['seq'=64,'chan'=4] {'chan','seq'}, dimensions={0} | all-to-all | bytes 1310720 | tf_op jit(solution)/shard_map/all_to_all | solution.py:238
  42.4 0.0 copy-done.3
  42.4 0.0 copy-done.4
  42.4 0.0 copy-done.5
  42.4 0.0 copy-done.6
  42.4 0.0 copy-done.7
  42.4 0.0 copy-done.8
  42.4 3.2 %shard_map.131 = bf16[2560,128]{1,0:T(8,128)(2,1)S(1)} custom-call(bf16[2560,128]{1,0:T(8,128)(2,1)S(1)} %bitcast.7, bf16[128,128]{1,0:T(8,128)(2,1)S(1)} %copy-done.8, bf16[128,256]{1,0:T(8,128)(2,1)S(1)} %copy-done.5, bf16[768,256]{1,0:T(8,128)(2,1)S(1)} %copy-done.4, bf16[768,256]{1,0:T(8,128)(2,1)S(1)} %copy-done.3, f32[64,128]{1,0:T(8,128)S(1)} %copy-done.7, ...), custom_call_target="tpu_custom_call" | custom-call | tf_op jit(solution)/shard_map/pallas_call | solution.py:222
  45.6 0.0 copy-start
  45.6 0.0 copy-start.1
  45.6 0.0 copy-start.2
  45.6 0.0 copy-start.9
  45.6 28.6 %all_to_all.11 = bf16[256,5,2,128]{3,2,1,0:T(2,128)(2,1)S(1)} all-to-all(bf16[256,5,2,128]{3,2,1,0:T(2,128)(2,1)S(1)} %bitcast.8), channel_id=1, replica_groups=mesh['seq'=64,'chan'=4] {'chan','seq'}, dimensions={0} | all-to-all | bytes 1310720 | tf_op jit(solution)/shard_map/all_to_all | solution.py:238
  74.3 0.0 copy-done
  74.3 0.0 copy-done.1
  74.3 0.0 copy-done.2
  74.3 0.0 copy-done.9
  74.3 1.1 %shard_map.132 = (bf16[128,1024]{1,0:T(8,128)(2,1)}, bf16[128,1024]{1,0:T(8,128)(2,1)}, f32[128,256]{1,0:T(8,128)}) custom-call(bf16[128,1024]{1,0:T(8,128)(2,1)S(1)} %copy-done.1, bf16[128,1024]{1,0:T(8,128)(2,1)S(1)} %copy-done.2, f32[128,1024]{1,0:T(8,128)S(1)} %copy-done, f32[1,1024]{1,0:T(1,128)S(1)} %bitcast.9, bf16[2560,128]{1,0:T(8,128)(2,1)S(1)} %bitcast.6), custom_call_target="tpu_custom_call" | custom-call | tf_op jit(solution)/shard_map/pallas_call | solution.py:222
Async XLA Ops:
  3.0 39.4 %copy-start.3 = (bf16[768,256]{1,0:T(8,128)(2,1)S(1)}, bf16[768,256]{1,0:T(8,128)(2,1)}, u32[]{:S(2)}) copy-start(bf16[768,256]{1,0:T(8,128)(2,1)} %constant.19.clone.inverse_ref) | copy-start | bytes 1179652
  3.0 39.4 %copy-start.4 = (bf16[768,256]{1,0:T(8,128)(2,1)S(1)}, bf16[768,256]{1,0:T(8,128)(2,1)}, u32[]{:S(2)}) copy-start(bf16[768,256]{1,0:T(8,128)(2,1)} %constant.18.clone.forward_ref) | copy-start | bytes 1179652
  3.0 39.4 %copy-start.5 = (bf16[128,256]{1,0:T(8,128)(2,1)S(1)}, bf16[128,256]{1,0:T(8,128)(2,1)}, u32[]{:S(2)}) copy-start(bf16[128,256]{1,0:T(8,128)(2,1)} %constant.17.clone.leave_ref) | copy-start | bytes 196612
  3.0 39.4 %copy-start.6 = (f32[64,128]{1,0:T(8,128)S(1)}, f32[64,128]{1,0:T(8,128)}, u32[]{:S(2)}) copy-start(f32[64,128]{1,0:T(8,128)} %constant.21.clone.sin_ref) | copy-start | bytes 98308
  3.0 39.4 %copy-start.7 = (f32[64,128]{1,0:T(8,128)S(1)}, f32[64,128]{1,0:T(8,128)}, u32[]{:S(2)}) copy-start(f32[64,128]{1,0:T(8,128)} %constant.20.clone.cos_ref) | copy-start | bytes 98308
  3.0 39.4 %copy-start.8 = (bf16[128,128]{1,0:T(8,128)(2,1)S(1)}, bf16[128,128]{1,0:T(8,128)(2,1)}, u32[]{:S(2)}) copy-start(bf16[128,128]{1,0:T(8,128)(2,1)} %constant.16.clone.enter_ref) | copy-start | bytes 98308
  45.6 28.7 %copy-start = (f32[128,1024]{1,0:T(8,128)S(1)}, f32[128,1024]{1,0:T(8,128)}, u32[]{:S(2)}) copy-start(f32[128,1024]{1,0:T(8,128)} %grad_ref.3) | copy-start | bytes 1572868
  45.6 28.7 %copy-start.1 = (bf16[128,1024]{1,0:T(8,128)(2,1)S(1)}, bf16[128,1024]{1,0:T(8,128)(2,1)}, u32[]{:S(2)}) copy-start(bf16[128,1024]{1,0:T(8,128)(2,1)} %values_ref.3) | copy-start | bytes 786436
  45.6 28.7 %copy-start.2 = (bf16[128,1024]{1,0:T(8,128)(2,1)S(1)}, bf16[128,1024]{1,0:T(8,128)(2,1)}, u32[]{:S(2)}) copy-start(bf16[128,1024]{1,0:T(8,128)(2,1)} %gates_ref.3) | copy-start | bytes 786436
  45.6 28.7 %copy-start.9 = (f32[1024]{0:T(1024)S(1)}, f32[1024]{0:T(1024)}, u32[]{:S(2)}) copy-start(f32[1024]{0:T(1024)} %param.15) | copy-start | bytes 12292

commit v8 on v7

--- a/solution.py
+++ b/solution.py
@@ -260,7 +260,7 @@
     sent = jax.ShapeDtypeStruct((pairs * LINES, rows), BF16)
     sent = call(
         pack_kernel,
-        sent,
+        pltpu.VMEM(sent.shape, BF16),
         (rank, values, gates, grad_out, filter_raw),
         [
             pltpu.VMEM((rows, width), BF16),
@@ -271,7 +271,7 @@
             pltpu.SemaphoreType.DMA((4,)),
         ],
         [scalar] + [pl.BlockSpec(memory_space=pltpu.HBM)] * 4,
-        limit=60,
+        limit=57,
     )
     back = exchange(transform(exchange(sent), blocks))
     shape = jax.ShapeDtypeStruct((rows, width), BF16)

time: 75.6 us -> 74.6 us (0.987)
  Pallas kernels: 6.64 us -> 5.81 us
    pallas_call x3, Pallas kernels: 6.64 us -> 5.81 us  [call(): pl.pallas_call(kernel, out_shape=out_shape, in_specs=specs or [VMEM] * le...]
where the time goes in v8:
time: 74.6 us; the launch traced here: 74.4 us
  blocking collectives  67.8 us (91%)
  Pallas kernels  5.81 us (8%)
  between operations  0.77 us (1%)
    all_to_all x2, blocking collectives, exchange(): lax.all_to_all(shaped, ('chan', 'seq'), split_axis=0, concat_axis=0, tile...  67.8 us
    pallas_call x3, Pallas kernels, call(): pl.pallas_call(kernel, out_shape=out_shape, in_specs=specs or [VMEM] * le...  5.81 us

profile of v8, /device:TPU:1, one launch (start us, length us, event | category | flops | bytes accessed | tf_op | source)
XLA Modules:
  0.0 74.4 jit_solution(17529825947621710021)
XLA Ops:
  0.6 1.5 %shard_map.130 = bf16[2560,128]{1,0:T(8,128)(2,1)S(1)} custom-call(s32[1]{0:T(128)} %bitcast.1.rank_ref, bf16[128,1024]{1,0:T(8,128)(2,1)} %values_ref.3, bf16[128,1024]{1,0:T(8,128)(2,1)} %gates_ref.3, f32[128,1024]{1,0:T(8,128)} %grad_ref.3, bf16[128,1024]{1,0:T(8,128)(2,1)} %filter_ref.1), custom_call_target="tpu_custom_call" | custom-call | tf_op jit(solution)/shard_map/pallas_call | solution.py:222
  2.1 0.0 copy-start.3
  2.2 0.0 copy-start.4
  2.2 0.0 copy-start.5
  2.2 0.0 copy-start.6
  2.2 0.0 copy-start.7
  2.2 0.0 copy-start.8
  2.2 39.1 %all_to_all.10 = bf16[256,5,2,128]{3,2,1,0:T(2,128)(2,1)S(1)} all-to-all(bf16[256,5,2,128]{3,2,1,0:T(2,128)(2,1)S(1)} %bitcast.7), channel_id=1, replica_groups=mesh['seq'=64,'chan'=4] {'chan','seq'}, dimensions={0} | all-to-all | bytes 1310720 | tf_op jit(solution)/shard_map/all_to_all | solution.py:238
  41.3 0.0 copy-done.3
  41.3 0.0 copy-done.4
  41.3 0.0 copy-done.5
  41.3 0.0 copy-done.6
  41.4 0.0 copy-done.7
  41.4 0.0 copy-done.8
  41.4 3.2 %shard_map.131 = bf16[2560,128]{1,0:T(8,128)(2,1)S(1)} custom-call(bf16[2560,128]{1,0:T(8,128)(2,1)S(1)} %bitcast.8, bf16[128,128]{1,0:T(8,128)(2,1)S(1)} %copy-done.8, bf16[128,256]{1,0:T(8,128)(2,1)S(1)} %copy-done.5, bf16[768,256]{1,0:T(8,128)(2,1)S(1)} %copy-done.4, bf16[768,256]{1,0:T(8,128)(2,1)S(1)} %copy-done.3, f32[64,128]{1,0:T(8,128)S(1)} %copy-done.7, ...), custom_call_target="tpu_custom_call" | custom-call | tf_op jit(solution)/shard_map/pallas_call | solution.py:222
  44.6 0.0 copy-start
  44.6 0.0 copy-start.1
  44.6 0.0 copy-start.2
  44.6 0.0 copy-start.9
  44.6 28.6 %all_to_all.11 = bf16[256,5,2,128]{3,2,1,0:T(2,128)(2,1)S(1)} all-to-all(bf16[256,5,2,128]{3,2,1,0:T(2,128)(2,1)S(1)} %bitcast.9), channel_id=1, replica_groups=mesh['seq'=64,'chan'=4] {'chan','seq'}, dimensions={0} | all-to-all | bytes 1310720 | tf_op jit(solution)/shard_map/all_to_all | solution.py:238
  73.2 0.0 copy-done
  73.3 0.0 copy-done.1
  73.3 0.0 copy-done.2
  73.3 0.0 copy-done.9
  73.3 1.1 %shard_map.132 = (bf16[128,1024]{1,0:T(8,128)(2,1)}, bf16[128,1024]{1,0:T(8,128)(2,1)}, f32[128,256]{1,0:T(8,128)}) custom-call(bf16[128,1024]{1,0:T(8,128)(2,1)S(1)} %copy-done.1, bf16[128,1024]{1,0:T(8,128)(2,1)S(1)} %copy-done.2, f32[128,1024]{1,0:T(8,128)S(1)} %copy-done, f32[1,1024]{1,0:T(1,128)S(1)} %bitcast.10, bf16[2560,128]{1,0:T(8,128)(2,1)S(1)} %bitcast.6), custom_call_target="tpu_custom_call" | custom-call | tf_op jit(solution)/shard_map/pallas_call | solution.py:222
Async XLA Ops:
  2.1 39.2 %copy-start.3 = (bf16[768,256]{1,0:T(8,128)(2,1)S(1)}, bf16[768,256]{1,0:T(8,128)(2,1)}, u32[]{:S(2)}) copy-start(bf16[768,256]{1,0:T(8,128)(2,1)} %constant.19.clone.inverse_ref) | copy-start | bytes 1179652
  2.2 39.2 %copy-start.4 = (bf16[768,256]{1,0:T(8,128)(2,1)S(1)}, bf16[768,256]{1,0:T(8,128)(2,1)}, u32[]{:S(2)}) copy-start(bf16[768,256]{1,0:T(8,128)(2,1)} %constant.18.clone.forward_ref) | copy-start | bytes 1179652
  2.2 39.2 %copy-start.5 = (bf16[128,256]{1,0:T(8,128)(2,1)S(1)}, bf16[128,256]{1,0:T(8,128)(2,1)}, u32[]{:S(2)}) copy-start(bf16[128,256]{1,0:T(8,128)(2,1)} %constant.17.clone.leave_ref) | copy-start | bytes 196612
  2.2 39.2 %copy-start.6 = (f32[64,128]{1,0:T(8,128)S(1)}, f32[64,128]{1,0:T(8,128)}, u32[]{:S(2)}) copy-start(f32[64,128]{1,0:T(8,128)} %constant.21.clone.sin_ref) | copy-start | bytes 98308
  2.2 39.2 %copy-start.7 = (f32[64,128]{1,0:T(8,128)S(1)}, f32[64,128]{1,0:T(8,128)}, u32[]{:S(2)}) copy-start(f32[64,128]{1,0:T(8,128)} %constant.20.clone.cos_ref) | copy-start | bytes 98308
  2.2 39.2 %copy-start.8 = (bf16[128,128]{1,0:T(8,128)(2,1)S(1)}, bf16[128,128]{1,0:T(8,128)(2,1)}, u32[]{:S(2)}) copy-start(bf16[128,128]{1,0:T(8,128)(2,1)} %constant.16.clone.enter_ref) | copy-start | bytes 98308
  44.6 28.7 %copy-start = (f32[128,1024]{1,0:T(8,128)S(1)}, f32[128,1024]{1,0:T(8,128)}, u32[]{:S(2)}) copy-start(f32[128,1024]{1,0:T(8,128)} %grad_ref.3) | copy-start | bytes 1572868
  44.6 28.7 %copy-start.1 = (bf16[128,1024]{1,0:T(8,128)(2,1)S(1)}, bf16[128,1024]{1,0:T(8,128)(2,1)}, u32[]{:S(2)}) copy-start(bf16[128,1024]{1,0:T(8,128)(2,1)} %values_ref.3) | copy-start | bytes 786436
  44.6 28.7 %copy-start.2 = (bf16[128,1024]{1,0:T(8,128)(2,1)S(1)}, bf16[128,1024]{1,0:T(8,128)(2,1)}, u32[]{:S(2)}) copy-start(bf16[128,1024]{1,0:T(8,128)(2,1)} %gates_ref.3) | copy-start | bytes 786436
  44.6 28.7 %copy-start.9 = (f32[1024]{0:T(1024)S(1)}, f32[1024]{0:T(1024)}, u32[]{:S(2)}) copy-start(f32[1024]{0:T(1024)} %param.15) | copy-start | bytes 12292

commit v9 on v8

--- a/solution.py
+++ b/solution.py
@@ -36,16 +36,13 @@
     inverse = np.block([[row_cos, row_sin], [-row_sin, row_cos]])
     enter_high, enter_low = split_pair(enter)
     leave_high, leave_low = split_pair(leave)
-    return (
-        np.concatenate([enter_high, enter_low], axis=1),
-        np.block([[leave_high, leave_high], [leave_low, np.zeros_like(leave_low)]]),
-        *(
-            np.concatenate([high, low, high], axis=0)
-            for high, low in (split_pair(forward), split_pair(inverse))
-        ),
-        np.cos(turn).astype(np.float32),
-        np.sin(turn).astype(np.float32),
-    )
+    wide = [
+        np.concatenate([high, low, high], axis=0)
+        for high, low in (split_pair(forward), split_pair(inverse))
+    ]
+    wide.append(np.block([[leave_high, leave_high], [leave_low, np.zeros_like(leave_low)]]))
+    turns = np.concatenate([np.cos(turn), np.sin(turn)], axis=0).astype(np.float32)
+    return np.concatenate([enter_high, enter_low], axis=1), np.concatenate(wide, axis=0), turns
 
 
 def split_value(x):
@@ -102,15 +99,16 @@
 
 
 def spectra_kernel(
-    in_ref, enter_ref, leave_ref, forward_ref, inverse_ref, cos_ref, sin_ref, out_ref, wide, result
+    in_ref, enter_ref, table_ref, turn_ref, out_ref, wide, result
 ):
-    blocks, rows = cos_ref.shape
+    blocks, rows = turn_ref.shape[0] // 2, turn_ref.shape[1]
+    deep = 6 * rows
     copies = in_ref.shape[0] // (blocks * LINES)
-    cos_t, sin_t = cos_ref[...], sin_ref[...]
+    cos_t, sin_t = turn_ref[:blocks, :], turn_ref[blocks:, :]
     wide[: in_ref.shape[0], :] = in_ref[...].astype(F32)
 
     def spectrum(starts):
-        table = forward_ref[...]
+        table = table_ref[:deep, :]
         step = len(starts) // PIECES
 
         def turn(first):
@@ -136,7 +134,7 @@
         return full[:, :rows], full[:, rows:]
 
     def signal(re, im):
-        table = inverse_ref[...]
+        table = table_ref[deep : 2 * deep, :]
         size = re.shape[0] // 4
         starts = list(range(0, re.shape[0], size))
 
@@ -153,7 +151,7 @@
         waiting, done = [], []
 
         def leave(x):
-            both = dot(leave_ref[...], x)
+            both = dot(table_ref[2 * deep :, :], x)
             mixed = both[:blocks] + both[blocks:]
             return [mixed[:, c : c + rows] for c in range(0, mixed.shape[1], rows)]
 
@@ -198,32 +196,42 @@
 
 
 def finish_kernel(
-    values_ref, gates_ref, grad_ref, skip_ref, in_ref, value_out, gate_out, filter_out, wide, flat
+    values_ref, gates_ref, grad_ref, skip_ref, in_ref, value_out, gate_out, filter_out, wide, value, gate, taps, sems
 ):
-    pairs = flat.shape[0] // SHARE
+    pairs = in_ref.shape[0] // LINES
     wide[: in_ref.shape[0], :] = in_ref[...].astype(F32)
-
-    def part(first):
-        for q in range(SHARE):
-            flat[q * pairs : (q + 1) * pairs, :] = wide[
-                pl.ds(first + q, pairs, stride=LINES), :
-            ]
-        return flat[...].T
-
-    grad = grad_ref[...]
-    skip = skip_ref[...]
-    gate_out[...] = (grad * (part(0) + skip * values_ref[...].astype(F32))).astype(BF16)
-    gate_term = (grad * gates_ref[...].astype(F32)).astype(BF16).astype(F32)
-    value_out[...] = (part(SHARE) + skip * gate_term).astype(BF16)
-    filter_out[...] = wide[pl.ds(2 * SHARE, pairs, stride=LINES), :].T
-
-
-def call(kernel, out_shape, args, scratch, specs=None, limit=48):
+    copies = []
+
+    def send(src, dst):
+        copy = pltpu.make_async_copy(src, dst, sems.at[len(copies)])
+        copy.start()
+        copies.append(copy)
+
+    taps[...] = wide[pl.ds(2 * SHARE, pairs, stride=LINES), :].T
+    send(taps, filter_out)
+    for q in range(SHARE):
+        cut = slice(q * pairs, (q + 1) * pairs)
+        grad, skip = grad_ref[:, cut], skip_ref[:, cut]
+        conv = wide[pl.ds(q, pairs, stride=LINES), :].T
+        gate[:, cut] = (grad * (conv + skip * values_ref[:, cut].astype(F32))).astype(BF16)
+    send(gate, gate_out)
+    for q in range(SHARE):
+        cut = slice(q * pairs, (q + 1) * pairs)
+        grad, skip = grad_ref[:, cut], skip_ref[:, cut]
+        back = wide[pl.ds(SHARE + q, pairs, stride=LINES), :].T
+        gate_term = (grad * gates_ref[:, cut].astype(F32)).astype(BF16).astype(F32)
+        value[:, cut] = (back + skip * gate_term).astype(BF16)
+    send(value, value_out)
+    for copy in copies:
+        copy.wait()
+
+
+def call(kernel, out_shape, args, scratch, specs=None, limit=48, out=VMEM):
     return pl.pallas_call(
         kernel,
         out_shape=out_shape,
         in_specs=specs or [VMEM] * len(args),
-        out_specs=jax.tree.map(lambda _: VMEM, out_shape),
+        out_specs=jax.tree.map(lambda _: out, out_shape),
         scratch_shapes=scratch,
         compiler_params=pltpu.CompilerParams(vmem_limit_bytes=limit * 1024 * 1024),
     )(*args)
@@ -255,7 +263,6 @@
     blocks = lax.axis_size("seq")
     pairs = blocks * lax.axis_size("chan")
     rank = lax.axis_index("chan").astype(jnp.int32).reshape(1)
-    flat = pltpu.VMEM((width, rows), F32)
     scalar = pl.BlockSpec(memory_space=pltpu.SMEM)
     sent = jax.ShapeDtypeStruct((pairs * LINES, rows), BF16)
     sent = call(
@@ -279,7 +286,14 @@
         finish_kernel,
         (shape, shape, jax.ShapeDtypeStruct((rows, width // lax.axis_size("chan")), F32)),
         (values, gates, grad_out, skip_gain[None, :], back),
-        [spare(back), flat],
+        [
+            spare(back),
+            pltpu.VMEM((rows, width), BF16),
+            pltpu.VMEM((rows, width), BF16),
+            pltpu.VMEM((rows, pairs), F32),
+            pltpu.SemaphoreType.DMA((3,)),
+        ],
+        out=pl.BlockSpec(memory_space=pltpu.HBM),
     )
 
 

time: 74.6 us -> 74.5 us (level)
  no operation moved by 1% of the time
where the time goes in v9:
time: 74.5 us; the launch traced here: 74.3 us
  blocking collectives  67.8 us (91%)
  Pallas kernels  5.78 us (8%)
    all_to_all x2, blocking collectives, exchange(): lax.all_to_all(shaped, ('chan', 'seq'), split_axis=0, concat_axis=0, tile...  67.8 us
    pallas_call x3, Pallas kernels, call(): pl.pallas_call(kernel, out_shape=out_shape, in_specs=specs or [VMEM] * le...  5.78 us

profile of v9, /device:TPU:1, one launch (start us, length us, event | category | flops | bytes accessed | tf_op | source)
XLA Modules:
  0.0 74.3 jit_solution(2806903610639313474)
XLA Ops:
  0.6 1.5 %shard_map.103 = bf16[2560,128]{1,0:T(8,128)(2,1)S(1)} custom-call(s32[1]{0:T(128)} %bitcast.1.rank_ref, bf16[128,1024]{1,0:T(8,128)(2,1)} %values_ref.3, bf16[128,1024]{1,0:T(8,128)(2,1)} %gates_ref.3, f32[128,1024]{1,0:T(8,128)} %grad_ref.3, bf16[128,1024]{1,0:T(8,128)(2,1)} %filter_ref.1), custom_call_target="tpu_custom_call" | custom-call | tf_op jit(solution)/shard_map/pallas_call | solution.py:230
  2.1 0.0 copy-start.3
  2.2 0.0 copy-start.4
  2.2 0.0 copy-start.5
  2.2 39.1 %all_to_all.10 = bf16[256,5,2,128]{3,2,1,0:T(2,128)(2,1)S(1)} all-to-all(bf16[256,5,2,128]{3,2,1,0:T(2,128)(2,1)S(1)} %bitcast.7), channel_id=1, replica_groups=mesh['seq'=64,'chan'=4] {'chan','seq'}, dimensions={0} | all-to-all | bytes 1310720 | tf_op jit(solution)/shard_map/all_to_all | solution.py:246
  41.3 0.0 copy-done.3
  41.3 0.0 copy-done.4
  41.3 0.0 copy-done.5
  41.3 3.2 %shard_map.104 = bf16[2560,128]{1,0:T(8,128)(2,1)S(1)} custom-call(bf16[2560,128]{1,0:T(8,128)(2,1)S(1)} %bitcast.8, bf16[128,128]{1,0:T(8,128)(2,1)S(1)} %copy-done.5, bf16[1664,256]{1,0:T(8,128)(2,1)S(1)} %copy-done.3, f32[128,128]{1,0:T(8,128)S(1)} %copy-done.4), custom_call_target="tpu_custom_call" | custom-call | tf_op jit(solution)/shard_map/pallas_call | solution.py:230
  44.5 0.0 copy-start
  44.5 0.0 copy-start.1
  44.5 0.0 copy-start.2
  44.5 0.0 copy-start.6
  44.5 28.6 %all_to_all.11 = bf16[256,5,2,128]{3,2,1,0:T(2,128)(2,1)S(1)} all-to-all(bf16[256,5,2,128]{3,2,1,0:T(2,128)(2,1)S(1)} %bitcast.9), channel_id=1, replica_groups=mesh['seq'=64,'chan'=4] {'chan','seq'}, dimensions={0} | all-to-all | bytes 1310720 | tf_op jit(solution)/shard_map/all_to_all | solution.py:246
  73.2 0.0 copy-done
  73.2 0.0 copy-done.1
  73.2 0.0 copy-done.2
  73.2 0.0 copy-done.6
  73.2 1.1 %shard_map.105 = (bf16[128,1024]{1,0:T(8,128)(2,1)}, bf16[128,1024]{1,0:T(8,128)(2,1)}, f32[128,256]{1,0:T(8,128)}) custom-call(bf16[128,1024]{1,0:T(8,128)(2,1)S(1)} %copy-done.1, bf16[128,1024]{1,0:T(8,128)(2,1)S(1)} %copy-done.2, f32[128,1024]{1,0:T(8,128)S(1)} %copy-done, f32[1,1024]{1,0:T(1,128)S(1)} %bitcast.10, bf16[2560,128]{1,0:T(8,128)(2,1)S(1)} %bitcast.6), custom_call_target="tpu_custom_call" | custom-call | tf_op jit(solution)/shard_map/pallas_call | solution.py:230
Async XLA Ops:
  2.1 39.2 %copy-start.3 = (bf16[1664,256]{1,0:T(8,128)(2,1)S(1)}, bf16[1664,256]{1,0:T(8,128)(2,1)}, u32[]{:S(2)}) copy-start(bf16[1664,256]{1,0:T(8,128)(2,1)} %constant.11.clone.table_ref) | copy-start | bytes 2555908
  2.2 39.1 %copy-start.4 = (f32[128,128]{1,0:T(8,128)S(1)}, f32[128,128]{1,0:T(8,128)}, u32[]{:S(2)}) copy-start(f32[128,128]{1,0:T(8,128)} %constant.12.clone.turn_ref) | copy-start | bytes 196612
  2.2 39.1 %copy-start.5 = (bf16[128,128]{1,0:T(8,128)(2,1)S(1)}, bf16[128,128]{1,0:T(8,128)(2,1)}, u32[]{:S(2)}) copy-start(bf16[128,128]{1,0:T(8,128)(2,1)} %constant.10.clone.enter_ref) | copy-start | bytes 98308
  44.5 28.7 %copy-start = (f32[128,1024]{1,0:T(8,128)S(1)}, f32[128,1024]{1,0:T(8,128)}, u32[]{:S(2)}) copy-start(f32[128,1024]{1,0:T(8,128)} %grad_ref.3) | copy-start | bytes 1572868
  44.5 28.7 %copy-start.1 = (bf16[128,1024]{1,0:T(8,128)(2,1)S(1)}, bf16[128,1024]{1,0:T(8,128)(2,1)}, u32[]{:S(2)}) copy-start(bf16[128,1024]{1,0:T(8,128)(2,1)} %values_ref.3) | copy-start | bytes 786436
  44.5 28.7 %copy-start.2 = (bf16[128,1024]{1,0:T(8,128)(2,1)S(1)}, bf16[128,1024]{1,0:T(8,128)(2,1)}, u32[]{:S(2)}) copy-start(bf16[128,1024]{1,0:T(8,128)(2,1)} %gates_ref.3) | copy-start | bytes 786436
  44.5 28.7 %copy-start.6 = (f32[1024]{0:T(1024)S(1)}, f32[1024]{0:T(1024)}, u32[]{:S(2)}) copy-start(f32[1024]{0:T(1024)} %param.12) | copy-start | bytes 12292

commit v10 on v9

--- a/solution.py
+++ b/solution.py
@@ -67,12 +67,14 @@
 
 def pack_kernel(rank_ref, values_ref, gates_ref, grad_ref, filter_ref, out_ref, values, gates, grad, taps, rows_ref, sems):
     pairs = out_ref.shape[0] // LINES
-    copies = [
-        pltpu.make_async_copy(src, dst, sems.at[k])
-        for k, (src, dst) in enumerate(
-            ((values_ref, values), (filter_ref, taps), (gates_ref, gates), (grad_ref, grad))
-        )
-    ]
+    cut = pl.ds(pl.multiple_of(rank_ref[0] * pairs, pairs), pairs)
+    moves = (
+        (values_ref, values),
+        (filter_ref.at[:, cut], taps),
+        (gates_ref, gates),
+        (grad_ref, grad),
+    )
+    copies = [pltpu.make_async_copy(src, dst, sems.at[k]) for k, (src, dst) in enumerate(moves)]
     for copy in copies:
         copy.start()
 
@@ -87,8 +89,7 @@
     copies[0].wait()
     place(values[...].astype(F32), 0)
     copies[1].wait()
-    start = pl.multiple_of(rank_ref[0] * pairs, pairs)
-    own = taps[:, pl.ds(start, pairs)].astype(F32).T
+    own = taps[...].astype(F32).T
     for line in range(2 * SHARE, LINES):
         put(line, own)
     copies[2].wait()
@@ -273,7 +274,7 @@
             pltpu.VMEM((rows, width), BF16),
             pltpu.VMEM((rows, width), BF16),
             pltpu.VMEM((rows, width), F32),
-            pltpu.VMEM((rows, width), BF16),
+            pltpu.VMEM((rows, pairs), BF16),
             spare(sent),
             pltpu.SemaphoreType.DMA((4,)),
         ],

time: 74.5 us -> 74.4 us (level)
  no operation moved by 1% of the time
where the time goes in v10:
time: 74.4 us; the launch traced here: 74.3 us
  blocking collectives  67.8 us (91%)
  Pallas kernels  5.74 us (8%)
    all_to_all x2, blocking collectives, exchange(): lax.all_to_all(shaped, ('chan', 'seq'), split_axis=0, concat_axis=0, tile...  67.8 us
    pallas_call x3, Pallas kernels, call(): pl.pallas_call(kernel, out_shape=out_shape, in_specs=specs or [VMEM] * le...  5.74 us

profile of v10, /device:TPU:1, one launch (start us, length us, event | category | flops | bytes accessed | tf_op | source)
XLA Modules:
  0.0 74.3 jit_solution(11051529030758136269)
XLA Ops:
  0.6 1.5 %shard_map.103 = bf16[2560,128]{1,0:T(8,128)(2,1)S(1)} custom-call(s32[1]{0:T(128)} %bitcast.1.rank_ref, bf16[128,1024]{1,0:T(8,128)(2,1)} %values_ref.3, bf16[128,1024]{1,0:T(8,128)(2,1)} %gates_ref.3, f32[128,1024]{1,0:T(8,128)} %grad_ref.3, bf16[128,1024]{1,0:T(8,128)(2,1)} %filter_ref.1), custom_call_target="tpu_custom_call" | custom-call | tf_op jit(solution)/shard_map/pallas_call | solution.py:231
  2.1 0.0 copy-start.3
  2.1 0.0 copy-start.4
  2.1 0.0 copy-start.5
  2.1 39.1 %all_to_all.10 = bf16[256,5,2,128]{3,2,1,0:T(2,128)(2,1)S(1)} all-to-all(bf16[256,5,2,128]{3,2,1,0:T(2,128)(2,1)S(1)} %bitcast.7), channel_id=1, replica_groups=mesh['seq'=64,'chan'=4] {'chan','seq'}, dimensions={0} | all-to-all | bytes 1310720 | tf_op jit(solution)/shard_map/all_to_all | solution.py:247
  41.2 0.0 copy-done.3
  41.3 0.0 copy-done.4
  41.3 0.0 copy-done.5
  41.3 3.2 %shard_map.104 = bf16[2560,128]{1,0:T(8,128)(2,1)S(1)} custom-call(bf16[2560,128]{1,0:T(8,128)(2,1)S(1)} %bitcast.8, bf16[128,128]{1,0:T(8,128)(2,1)S(1)} %copy-done.5, bf16[1664,256]{1,0:T(8,128)(2,1)S(1)} %copy-done.3, f32[128,128]{1,0:T(8,128)S(1)} %copy-done.4), custom_call_target="tpu_custom_call" | custom-call | tf_op jit(solution)/shard_map/pallas_call | solution.py:231
  44.5 0.0 copy-start
  44.5 0.0 copy-start.1
  44.5 0.0 copy-start.2
  44.5 0.0 copy-start.6
  44.5 28.6 %all_to_all.11 = bf16[256,5,2,128]{3,2,1,0:T(2,128)(2,1)S(1)} all-to-all(bf16[256,5,2,128]{3,2,1,0:T(2,128)(2,1)S(1)} %bitcast.9), channel_id=1, replica_groups=mesh['seq'=64,'chan'=4] {'chan','seq'}, dimensions={0} | all-to-all | bytes 1310720 | tf_op jit(solution)/shard_map/all_to_all | solution.py:247
  73.2 0.0 copy-done
  73.2 0.0 copy-done.1
  73.2 0.0 copy-done.2
  73.2 0.0 copy-done.6
  73.2 1.1 %shard_map.105 = (bf16[128,1024]{1,0:T(8,128)(2,1)}, bf16[128,1024]{1,0:T(8,128)(2,1)}, f32[128,256]{1,0:T(8,128)}) custom-call(bf16[128,1024]{1,0:T(8,128)(2,1)S(1)} %copy-done.1, bf16[128,1024]{1,0:T(8,128)(2,1)S(1)} %copy-done.2, f32[128,1024]{1,0:T(8,128)S(1)} %copy-done, f32[1,1024]{1,0:T(1,128)S(1)} %bitcast.10, bf16[2560,128]{1,0:T(8,128)(2,1)S(1)} %bitcast.6), custom_call_target="tpu_custom_call" | custom-call | tf_op jit(solution)/shard_map/pallas_call | solution.py:231
Async XLA Ops:
  2.1 39.2 %copy-start.3 = (bf16[1664,256]{1,0:T(8,128)(2,1)S(1)}, bf16[1664,256]{1,0:T(8,128)(2,1)}, u32[]{:S(2)}) copy-start(bf16[1664,256]{1,0:T(8,128)(2,1)} %constant.11.clone.table_ref) | copy-start | bytes 2555908
  2.1 39.1 %copy-start.4 = (f32[128,128]{1,0:T(8,128)S(1)}, f32[128,128]{1,0:T(8,128)}, u32[]{:S(2)}) copy-start(f32[128,128]{1,0:T(8,128)} %constant.12.clone.turn_ref) | copy-start | bytes 196612
  2.1 39.1 %copy-start.5 = (bf16[128,128]{1,0:T(8,128)(2,1)S(1)}, bf16[128,128]{1,0:T(8,128)(2,1)}, u32[]{:S(2)}) copy-start(bf16[128,128]{1,0:T(8,128)(2,1)} %constant.10.clone.enter_ref) | copy-start | bytes 98308
  44.5 28.7 %copy-start = (f32[128,1024]{1,0:T(8,128)S(1)}, f32[128,1024]{1,0:T(8,128)}, u32[]{:S(2)}) copy-start(f32[128,1024]{1,0:T(8,128)} %grad_ref.3) | copy-start | bytes 1572868
  44.5 28.7 %copy-start.1 = (bf16[128,1024]{1,0:T(8,128)(2,1)S(1)}, bf16[128,1024]{1,0:T(8,128)(2,1)}, u32[]{:S(2)}) copy-start(bf16[128,1024]{1,0:T(8,128)(2,1)} %values_ref.3) | copy-start | bytes 786436
  44.5 28.7 %copy-start.2 = (bf16[128,1024]{1,0:T(8,128)(2,1)S(1)}, bf16[128,1024]{1,0:T(8,128)(2,1)}, u32[]{:S(2)}) copy-start(bf16[128,1024]{1,0:T(8,128)(2,1)} %gates_ref.3) | copy-start | bytes 786436
  44.5 28.7 %copy-start.6 = (f32[1024]{0:T(1024)S(1)}, f32[1024]{0:T(1024)}, u32[]{:S(2)}) copy-start(f32[1024]{0:T(1024)} %param.12) | copy-start | bytes 12292
